TPU v7x, 32 devices: a whole 2x2x4 slice. The times are simulated.
32 devices in a mesh: seq: 8 (over y, x, core), exp: 4 (over z).
Axes of the slice: x: 2, y: 2, z: 4, core: 2. Of those that a mesh axis runs over, the one named last changes fastest.
Arguments:
- inputs: bfloat16 [4, 4096, 768], P('exp', 'seq'), may hold values from -6 to 6
- token_ids: int32 [4, 4096], P('exp', 'seq'), may hold values from 0 to 50256, as said below
- hash_table: int32 [50257], replicated, may hold values from 0 to 3
- capacity: int32 [4], replicated, may hold values from 80 to 160, as said below
- ln1_gain: float32 [768], replicated, may hold values from 0.5 to 1.5
- ln1_bias: float32 [768], replicated, may hold values from -0.6 to 0.6
- w_qkv: bfloat16 [768, 2304], replicated, may hold values from -0.21875 to 0.21875
- q_bias: float32 [768], replicated, may hold values from -0.6 to 0.6
- v_bias: float32 [768], replicated, may hold values from -0.6 to 0.6
- w_out: bfloat16 [768, 768], replicated, may hold values from -0.875 to 0.875
- out_bias: float32 [768], replicated, may hold values from -0.6 to 0.6
- ln2_gain: float32 [768], replicated, may hold values from 0.5 to 1.5
- ln2_bias: float32 [768], replicated, may hold values from -0.6 to 0.6
- up_weight: bfloat16 [4, 768, 3072], P('exp'), may hold values from -0.21875 to 0.21875
- up_bias: float32 [4, 3072], P('exp'), may hold values from -0.6 to 0.6
- down_weight: bfloat16 [4, 3072, 768], P('exp'), may hold values from -0.109375 to 0.109375
- down_bias: float32 [4, 768], P('exp'), may hold values from -0.6 to 0.6
- out_grad: bfloat16 [4, 4096, 768], P('exp', 'seq'), may hold values from -6 to 6
Outputs:
- output: bfloat16 [4, 4096, 768], P('exp', 'seq')
- input_grad: float32 [4, 4096, 768], P('exp', 'seq')
- ln1_gain_grad: float32 [768], replicated
- ln1_bias_grad: float32 [768], replicated
- w_qkv_grad: float32 [768, 2304], replicated
- q_bias_grad: float32 [768], replicated
- v_bias_grad: float32 [768], replicated
- w_out_grad: float32 [768, 768], replicated
- out_bias_grad: float32 [768], replicated
- ln2_gain_grad: float32 [768], replicated
- ln2_bias_grad: float32 [768], replicated
- up_weight_grad: float32 [4, 768, 3072], P('exp', None, 'seq')
- up_bias_grad: float32 [4, 3072], P('exp', 'seq')
- down_weight_grad: float32 [4, 3072, 768], P('exp', 'seq')
- down_bias_grad: float32 [4, 768], P('exp', 'seq')
Inputs may be any that keep to these rules, and one draw needn't show every extreme that they name: `token_ids`: ids of one device's block are heavy-tailed: one id, which hash_table sends to an expert of capacity 160, fills between 160 and 320 positions of every block. Some expert has capacity exactly 160.
All inputs are finite; a program needn't handle non-finite values.
Results may differ from a plain program's by a relative error of at most 0.025.
Values may be sent and summed in bfloat16 or wider, within the bound.
No kernel may reach another device: no remote copies, remote signals or barrier semaphores. Data moves between devices by JAX's collectives and lax.ppermute only.
A program may use at most 384 MiB of HBM per device.

v0:
```python
from functools import partial
import math

import jax
import jax.numpy as jnp
from jax import lax
from jax.sharding import PartitionSpec as P

HEADS = 12


norm_eps = 1e-05
logit_scale = 0.125
masked_score = -1e30


def shortened(shard):

    def short(part):
        return part.astype(jnp.bfloat16) if part.dtype == jnp.float32 else part

    return jax.tree.map(short, shard)


def passed_along(block, axis, distance):
    devices = range(lax.axis_size(axis))
    route = [((i - distance) % len(devices), i) for i in devices]
    return lax.ppermute(block, axis, route)


def layer_norm(values, gain, shift):
    centre = jnp.mean(values, axis=-1, keepdims=True)
    centered = values - centre
    spread = jnp.mean(centered * centered, axis=-1, keepdims=True)
    return centered * lax.rsqrt(spread + norm_eps) * gain + shift


def smooth_unit(values):
    return jax.nn.gelu(values, approximate=False)


def smooth_slope(values):
    normal_cdf = 0.5 * (1.0 + jax.scipy.special.erf(values * (1.0 / math.sqrt(2.0))))
    normal_pdf = jnp.exp(-0.5 * values * values) * (1.0 / math.sqrt(2.0 * math.pi))
    return normal_cdf + values * normal_pdf


def scores_at(queries, keys_part, query_start, key_start):
    raw = (
        jnp.einsum("bqhd,bkhd->bhqk", queries, keys_part, preferred_element_type=jnp.float32)
        * logit_scale
    )
    query_place = query_start + lax.iota(jnp.int32, queries.shape[1])
    key_place = key_start + lax.iota(jnp.int32, keys_part.shape[1])
    return jnp.where(key_place[None, :] <= query_place[:, None], raw, masked_score)


def block_scores(queries, keys_part, query_owner, key_owner):
    span = queries.shape[1]
    return scores_at(queries, keys_part, query_owner * span, key_owner * span)


def attend_block(state, queries, keys_part, values_part, query_owner, key_owner):
    run_max, run_sum, total = state
    scores = block_scores(queries, keys_part, query_owner, key_owner)
    new_max = jnp.maximum(run_max, jnp.max(scores, axis=-1))
    factor = jnp.exp(run_max - new_max)
    weights = jnp.exp(scores - new_max[..., None])
    run_sum = run_sum * factor + jnp.sum(weights, axis=-1)
    update = jnp.einsum(
        "bhqk,bkhd->bqhd",
        weights.astype(jnp.bfloat16),
        values_part,
        preferred_element_type=jnp.float32,
    )
    total = total * jnp.swapaxes(factor, 1, 2)[..., None] + update
    return (new_max, run_sum, total)


def grads_at(
    queries, grad_attn, lse_part, delta_part, keys_part, values_part, query_start, key_start
):
    scores = scores_at(queries, keys_part, query_start, key_start)
    probs = jnp.exp(scores - lse_part[..., None])
    grad_values = jnp.einsum(
        "bhqk,bqhd->bkhd", probs.astype(jnp.bfloat16), grad_attn, preferred_element_type=jnp.float32
    )
    grad_probs = jnp.einsum(
        "bqhd,bkhd->bhqk", grad_attn, values_part, preferred_element_type=jnp.float32
    )
    grad_scores = (probs * (grad_probs - delta_part[..., None])).astype(jnp.bfloat16)
    grad_queries = (
        jnp.einsum("bhqk,bkhd->bqhd", grad_scores, keys_part, preferred_element_type=jnp.float32)
        * logit_scale
    )
    grad_keys = (
        jnp.einsum("bhqk,bqhd->bkhd", grad_scores, queries, preferred_element_type=jnp.float32)
        * logit_scale
    )
    return (grad_queries, grad_keys, grad_values)


def block_grads(
    queries, grad_attn, lse_part, delta_part, keys_part, values_part, query_owner, key_owner
):
    span = queries.shape[1]
    return grads_at(
        queries,
        grad_attn,
        lse_part,
        delta_part,
        keys_part,
        values_part,
        query_owner * span,
        key_owner * span,
    )


def expert_forward(rows, up_weight, up_bias, down_weight, down_bias):
    count, senders, items, width = rows.shape
    flat = rows.reshape(count, senders * items, width)
    pre = (
        jnp.einsum("erd,edf->erf", flat, up_weight, preferred_element_type=jnp.float32)
        + up_bias[:, None, :]
    )
    hidden = smooth_unit(pre).astype(jnp.bfloat16)
    result = (
        jnp.einsum("erf,efd->erd", hidden, down_weight, preferred_element_type=jnp.float32)
        + down_bias[:, None, :]
    )
    return (rows, result.astype(jnp.bfloat16).reshape(count, senders, items, width))


def expert_backward(rows, grads, up_weight, up_bias, down_weight):
    count, senders, items, width = rows.shape
    flat = rows.reshape(count, senders * items, width)
    flat_grad = grads.reshape(count, senders * items, width)
    pre = (
        jnp.einsum("erd,edf->erf", flat, up_weight, preferred_element_type=jnp.float32)
        + up_bias[:, None, :]
    )
    hidden = smooth_unit(pre).astype(jnp.bfloat16)
    grad_down = jnp.einsum("erf,erd->efd", hidden, flat_grad, preferred_element_type=jnp.float32)
    grad_down_bias = jnp.sum(flat_grad, axis=1, dtype=jnp.float32)
    grad_hidden = jnp.einsum(
        "erd,efd->erf", flat_grad, down_weight, preferred_element_type=jnp.float32
    )
    grad_pre = (grad_hidden * smooth_slope(pre)).astype(jnp.bfloat16)
    grad_up = jnp.einsum("erd,erf->edf", flat, grad_pre, preferred_element_type=jnp.float32)
    grad_up_bias = jnp.sum(grad_pre, axis=1, dtype=jnp.float32)
    grad_rows = jnp.einsum("erf,edf->erd", grad_pre, up_weight, preferred_element_type=jnp.float32)
    return (
        grad_up,
        grad_up_bias,
        grad_down,
        grad_down_bias,
        grad_rows.astype(jnp.bfloat16).reshape(rows.shape),
    )


def rotate_queries(carry):
    return jax.tree.map(
        lambda part, own: part.astype(own.dtype), passed_along(shortened(carry), "seq", 1), carry
    )


def local(
    inputs,
    token_ids,
    hash_table,
    capacity,
    ln1_gain,
    ln1_bias,
    w_qkv,
    q_bias,
    v_bias,
    w_out,
    out_bias,
    ln2_gain,
    ln2_bias,
    up_weight,
    up_bias,
    down_weight,
    down_bias,
    out_grad,
):
    nseq, span, width = inputs.shape
    tokens = nseq * span
    heads = HEADS
    head_dim = width // heads
    cycle = lax.axis_size("seq")
    place = lax.axis_index("seq")
    shape4 = (nseq, span, heads, head_dim)
    x_rows = inputs.reshape(tokens, width).astype(jnp.float32)
    normed, norm1_back = jax.vjp(layer_norm, x_rows, ln1_gain, ln1_bias)
    normed_low = normed.astype(jnp.bfloat16)
    projected = jnp.dot(normed_low, w_qkv, preferred_element_type=jnp.float32)
    queries = (projected[:, :width] + q_bias).astype(jnp.bfloat16).reshape(shape4)
    keys_own = projected[:, width : 2 * width].astype(jnp.bfloat16).reshape(shape4)
    values_own = (projected[:, 2 * width :] + v_bias).astype(jnp.bfloat16).reshape(shape4)
    start = (
        jnp.full((nseq, heads, span), masked_score, jnp.float32),
        jnp.zeros((nseq, heads, span), jnp.float32),
        jnp.zeros(shape4, jnp.float32),
    )
    state = attend_block(start, queries, keys_own, values_own, place, place)

    def forward_step(step, carry):
        moved = rotate_queries(carry)
        inner = attend_block(
            moved[1:], moved[0], keys_own, values_own, (place - step) % cycle, place
        )
        return (moved[0],) + tuple(inner)

    carried = lax.fori_loop(1, cycle, forward_step, (queries,) + tuple(state))
    _, run_max, run_sum, total = rotate_queries(carried)
    attn_full = total / jnp.swapaxes(run_sum, 1, 2)[..., None]
    lse = run_max + jnp.log(run_sum)
    attn_low = attn_full.astype(jnp.bfloat16).reshape(tokens, width)
    middle = x_rows + jnp.dot(attn_low, w_out, preferred_element_type=jnp.float32) + out_bias
    normed2, norm2_back = jax.vjp(layer_norm, middle, ln2_gain, ln2_bias)
    normed2_low = normed2.astype(jnp.bfloat16)
    experts = capacity.shape[0]
    cap = 5 * tokens // (4 * experts)
    expert_of = jnp.take(hash_table, token_ids.reshape(tokens))
    onehot = (expert_of[:, None] == lax.iota(jnp.int32, experts)[None, :]).astype(jnp.int32)
    rank = jnp.sum(onehot * (jnp.cumsum(onehot, axis=0) - 1), axis=1)
    kept = rank < jnp.take(capacity, expert_of)
    slot = jnp.where(kept, expert_of * cap + rank, experts * cap)
    fetch = jnp.minimum(slot, experts * cap - 1)
    outgoing = (
        jnp.zeros((experts * cap, width), jnp.bfloat16).at[slot].set(normed2_low, mode="drop")
    )
    outgoing = outgoing.reshape(experts, 1, cap, width)
    expert_work = partial(
        expert_forward,
        up_weight=up_weight,
        up_bias=up_bias,
        down_weight=down_weight,
        down_bias=down_bias,
    )
    received, produced = expert_work(
        lax.all_to_all(outgoing, "exp", split_axis=0, concat_axis=1, tiled=True)
    )
    returned = lax.all_to_all(produced, "exp", split_axis=1, concat_axis=0, tiled=True).reshape(
        experts * cap, width
    )
    expert_rows = jnp.where(
        kept[:, None], jnp.take(returned, fetch, axis=0).astype(jnp.float32), 0.0
    )
    output = (middle + expert_rows).astype(jnp.bfloat16).reshape(nseq, span, width)
    grad_rows = out_grad.reshape(tokens, width)
    grad_outgoing = (
        jnp.zeros((experts * cap, width), jnp.bfloat16).at[slot].set(grad_rows, mode="drop")
    )
    grad_outgoing = grad_outgoing.reshape(experts, 1, cap, width)
    grad_received = lax.all_to_all(grad_outgoing, "exp", split_axis=0, concat_axis=1, tiled=True)
    grad_up, grad_up_bias, grad_down, grad_down_bias, grad_tokens = expert_backward(
        received, grad_received, up_weight, up_bias, down_weight
    )
    grad_sent = lax.all_to_all(grad_tokens, "exp", split_axis=1, concat_axis=0, tiled=True).reshape(
        experts * cap, width
    )
    grad_normed2 = jnp.where(
        kept[:, None], jnp.take(grad_sent, fetch, axis=0).astype(jnp.float32), 0.0
    )
    grad_mid_norm, grad_ln2_gain, grad_ln2_bias = norm2_back(grad_normed2)
    grad_middle = grad_rows.astype(jnp.float32) + grad_mid_norm
    grad_branch = grad_middle.astype(jnp.bfloat16)
    grad_w_out = lax.dot_general(
        attn_low, grad_branch, (((0,), (0,)), ((), ())), preferred_element_type=jnp.float32
    )
    grad_out_bias = jnp.sum(grad_branch, axis=0, dtype=jnp.float32)
    grad_attn = lax.dot_general(
        grad_branch, w_out, (((1,), (1,)), ((), ())), preferred_element_type=jnp.float32
    )
    grad_attn = grad_attn.astype(jnp.bfloat16).reshape(shape4)
    delta = jnp.swapaxes(jnp.sum(grad_attn.astype(jnp.float32) * attn_full, axis=-1), 1, 2)
    zero_block = jnp.zeros(shape4, jnp.float32)
    gathered_keys, gathered_values = (
        lax.all_gather(keys_own, "seq", axis=1, tiled=True),
        lax.all_gather(values_own, "seq", axis=1, tiled=True),
    )

    def query_piece(owner, query_total):
        keys_part = lax.dynamic_slice_in_dim(gathered_keys, owner * span, span, 1)
        values_part = lax.dynamic_slice_in_dim(gathered_values, owner * span, span, 1)
        grad_q, _, _ = block_grads(
            queries, grad_attn, lse, delta, keys_part, values_part, place, owner
        )
        return query_total + grad_q

    grad_queries = lax.fori_loop(0, cycle, query_piece, zero_block)
    keys_part = gathered_keys
    values_part = gathered_values
    _, grad_k, grad_v = grads_at(
        queries, grad_attn, lse, delta, keys_part, values_part, place * span, jnp.int32(0)
    )
    key_sums = (
        lax.psum_scatter(
            jnp.concatenate([grad_k, grad_v], axis=3).transpose(1, 0, 2, 3).astype(jnp.bfloat16),
            "seq",
            scatter_dimension=0,
            tiled=True,
        )
        .astype(jnp.float32)
        .transpose(1, 0, 2, 3)
    )
    grad_keys = key_sums[..., :head_dim]
    grad_values = key_sums[..., head_dim:]
    grad_proj = jnp.concatenate(
        [
            grad_queries.reshape(tokens, width),
            grad_keys.reshape(tokens, width),
            grad_values.reshape(tokens, width),
        ],
        axis=1,
    ).astype(jnp.bfloat16)
    grad_w_qkv = lax.dot_general(
        normed_low, grad_proj, (((0,), (0,)), ((), ())), preferred_element_type=jnp.float32
    )
    grad_q_bias = jnp.sum(grad_proj[:, :width], axis=0, dtype=jnp.float32)
    grad_v_bias = jnp.sum(grad_proj[:, 2 * width :], axis=0, dtype=jnp.float32)
    grad_normed = lax.dot_general(
        grad_proj, w_qkv, (((1,), (1,)), ((), ())), preferred_element_type=jnp.float32
    )
    grad_from_norm, grad_ln1_gain, grad_ln1_bias = norm1_back(grad_normed)
    input_grad = (grad_middle + grad_from_norm).reshape(nseq, span, width)
    up_sum, up_bias_sum, down_sum, down_bias_sum = (
        lax.psum_scatter(
            grad_up.astype(jnp.bfloat16), "seq", scatter_dimension=2, tiled=True
        ).astype(jnp.float32),
        lax.psum_scatter(
            grad_up_bias.astype(jnp.bfloat16), "seq", scatter_dimension=1, tiled=True
        ).astype(jnp.float32),
        lax.psum_scatter(
            grad_down.astype(jnp.bfloat16), "seq", scatter_dimension=1, tiled=True
        ).astype(jnp.float32),
        lax.psum_scatter(
            grad_down_bias.astype(jnp.bfloat16), "seq", scatter_dimension=1, tiled=True
        ).astype(jnp.float32),
    )
    dense = lax.psum(
        (
            grad_ln1_gain,
            grad_ln1_bias,
            grad_w_qkv,
            grad_q_bias,
            grad_v_bias,
            grad_w_out,
            grad_out_bias,
            grad_ln2_gain,
            grad_ln2_bias,
        ),
        ("seq", "exp"),
    )
    return (
        output,
        input_grad,
        dense[0],
        dense[1],
        dense[2],
        dense[3],
        dense[4],
        dense[5],
        dense[6],
        dense[7],
        dense[8],
        up_sum,
        up_bias_sum,
        down_sum,
        down_bias_sum,
    )


def solution(mesh):
    in_specs = (
        P("exp", "seq", None),
        P("exp", "seq"),
        P(),
        P(),
        P(),
        P(),
        P(),
        P(),
        P(),
        P(),
        P(),
        P(),
        P(),
        P("exp", None, None),
        P("exp", None),
        P("exp", None, None),
        P("exp", None),
        P("exp", "seq", None),
    )
    out_specs = (
        P("exp", "seq", None),
        P("exp", "seq", None),
        P(),
        P(),
        P(),
        P(),
        P(),
        P(),
        P(),
        P(),
        P(),
        P("exp", None, "seq"),
        P("exp", "seq"),
        P("exp", "seq", None),
        P("exp", "seq"),
    )
    return jax.shard_map(local, mesh=mesh, in_specs=in_specs, out_specs=out_specs, check_vma=False)
```

profile of v0, /device:TPU:0, one launch (start us, length us, event | category | flops | bytes accessed | tf_op | source)
XLA Modules:
  0.0 1069.5 jit_solution(4464967130205000116)
XLA Ops:
  26.8 8.0 fusion.51
  40.4 7.3 fusion.53
  49.5 5.8 bitcast_add_fusion.3
  55.2 207.0 %while.37 = (s32[]{:T(128)}, bf16[1,512,12,64]{1,3,2,0:T(8,128)(2,1)}, f32[1,12,512]{2,1,0:T(8,128)}, bf16[1,12,512]{2,1,0:T(8,128)(2,1)}, bf16[1,512,12,64]{1,3...) while((s32[]{:T(128)}, ...), condition=%wide.region_7.8_spmd, body=%wide.region_4.7_spmd.sunk | while | flops 841794560 | bytes 52179432 | solution.py:215
  61.8 13.7 %collective-permute-done = bf16[1,512,12,64]{1,3,2,0:T(8,128)(2,1)} collective-permute-done((bf16[1,512,12,64]{1,3,2,0:T(8,128)(2,1)}, bf16[1,512,12,64]{1,3,2,0:T(8,128)(2,1)}, u32[]{:S(2)}, u32[]{:S(2)}) %collective-permute-start) | collective-permute-done | bytes 786464 | tf_op jit(solution)/shard_map/while/body/eval_jaxpr/ppermute | solution.py:28
  95.2 8.8 collective-permute-done
  123.7 8.8 collective-permute-done
  152.2 8.8 collective-permute-done
  180.7 8.8 collective-permute-done
  209.2 8.8 collective-permute-done
  237.6 8.8 collective-permute-done
  302.5 15.8 %all-to-all-done = bf16[4,1,160,768]{3,2,1,0:T(8,128)(2,1)} async-done(((bf16[4,1,160,768]{3,2,1,0:T(8,128)(2,1)}), bf16[4,1,160,768]{3,2,1,0:T(8,128)(2,1)}, u32[]{:S(2)}, u32[]{:S(2)}) %all-to-all-start) | async-done | bytes 983072 | tf_op jit(solution)/shard_map/all_to_all | solution.py:243
  322.8 22.7 %fusion.56 = (bf16[640,3072]{1,0:T(8,128)(2,1)S(1)}, f32[640,3072]{1,0:T(8,128)}) fusion(f32[3072]{0:T(1024)} %bitcast.369, bf16[640,768]{1,0:T(8,128)(2,1)} %bitcast.42, bf16[1,768,3072]{2,1,0:T(8,128)(2,1)} %param.37), kind=kOutput, calls=%fused_computation.72 | convolution fusion | flops 3149660160 | bytes 17510400 | tf_op jit(solution)/shard_map/erd,edf->erf/dot_general | solution.py:123
  347.3 6.5 add_convert_fusion
  358.9 9.3 fusion.161
  370.1 6.6 fusion.117
  376.7 5.5 all-to-all-done.1
  397.0 13.4 %all-to-all-done.3 = bf16[1,4,160,768]{3,2,0,1:T(8,128)(2,1)} async-done(((bf16[1,4,160,768]{3,2,0,1:T(8,128)(2,1)}), bf16[1,4,160,768]{3,2,0,1:T(8,128)(2,1)}, u32[]{:S(2)}, u32[]{:S(2)}) %all-to-all-start.3) | async-done | bytes 983072 | tf_op jit(solution)/shard_map/all_to_all | solution.py:261
  430.6 37.3 %fusion.75 = f32[12,512,4096]{2,1,0:T(8,128)} fusion(bf16[512,12,64]{0,2,1:T(8,128)(2,1)} %bitcast.325, bf16[1,4096,12,64]{1,3,2,0:T(8,128)(2,1)} %all-gather.3.cloned.1.call-done), kind=kOutput, calls=%fused_computation.96 | convolution fusion | flops 3221225472 | bytes 107741184 | tf_op jit(solution)/shard_map/bqhd,bkhd->bhqk/dot_general | solution.py:50
  467.9 39.7 %fusion.80 = bf16[1,4096,12,64]{1,3,2,0:T(8,128)(2,1)} fusion(bf16[512,12,64]{0,2,1:T(8,128)(2,1)} %bitcast.340, f32[12,512,4096]{2,1,0:T(8,128)} %fusion.75, f32[12,512]{1,0:T(8,128)} %get-tuple-element.562, pred[512,4096]{1,0:T(8,128)(4,1)} %iota_compare_fusion), kind=kOutput, calls=%fused_computation.100 | convolution fusion | flops 3325034496 | bytes 109862912 | tf_op jit(solution)/shard_map/bhqk,bqhd->bkhd/dot_general | solution.py:85
  507.6 52.0 %fusion.83 = bf16[1,4096,12,64]{1,3,2,0:T(8,128)(2,1)} fusion(bf16[512,12,64]{0,2,1:T(8,128)(2,1)} %bitcast.326, f32[12,512,4096]{2,1,0:T(8,128)} %fusion.75, f32[12,512]{1,0:T(8,128)} %bitcast.356, f32[12,512]{1,0:T(8,128)} %get-tuple-element.562, pred[512,4096]{1,0:T(8,128)(4,1)} %iota_compare_fusion, bf16[512,12,64]{0,2,1:T(8,128)(2,1)} %bitcast.341, ...), kind=kOutput, calls=%fused_computation.101 | convolution fusion | flops 6599737344 | bytes 116965376 | tf_op jit(solution)/shard_map/bhqk,bqhd->bkhd/dot_general | solution.py:97
  559.6 10.5 maximum_bitcast_fusion
  574.1 9.2 fusion.93
  583.3 20.8 %copy.76 = bf16[1,768,3072]{1,0,2:T(2,128)(2,1)} copy(bf16[1,768,3072]{2,1,0:T(8,128)(2,1)} %fusion.93) | data formatting | bytes 9437184
  604.1 6.6 copy.86
  610.8 8.7 fusion.94
  623.4 167.2 %while.38 = (s32[]{:T(128)}, f32[1,512,12,64]{1,3,2,0:T(8,128)}, bf16[1,4096,12,64]{1,3,2,0:T(8,128)(2,1)}, s32[]{:T(128)}, bf16[1,512,12,64]{1,3,2,0:T(8,128)(2...) while((s32[]{:T(128)}, f32[1,512,12,64]{1,3,2,0:T(8,128)}, ...), condition=%wide.region_19.21_spmd.clone, body=%wide.region_18.20_spmd.clone.sunk | while | flops 1228276736 | bytes 32843464 | solution.py:293
  624.4 7.8 fusion.214
  632.1 11.7 %bitcast_add_fusion.10 = f32[1,512,12,64]{1,3,2,0:T(8,128)} fusion(f32[1,512,12,64]{1,3,2,0:T(8,128)} %get-tuple-element.756, f32[12,512,512]{2,1,0:T(8,128)} %fusion.214, f32[12,512]{1,0:T(8,128)} %bitcast.358, f32[12,512]{1,0:T(8,128)} %bitcast.355, pred[512,512]{0,1:T(8,128)(4,1)} %broadcast_compare_fusion.6, ...), kind=kOutput, calls=%fused_computation.35.clone.1 | convolution fusion | flops 825360384 | bytes 18417152 | tf_op jit(solution)/shard_map/while/body/eval_jaxpr/bhqk,bkhd->bqhd/dot_general | solution.py:93
  644.8 7.7 fusion.214
  652.5 12.3 %bitcast_add_fusion.10 = f32[1,512,12,64]{1,3,2,0:T(8,128)} fusion(f32[1,512,12,64]{1,3,2,0:T(8,128)} %get-tuple-element.756, f32[12,512,512]{2,1,0:T(8,128)} %fusion.214, f32[12,512]{1,0:T(8,128)} %bitcast.358, f32[12,512]{1,0:T(8,128)} %bitcast.355, pred[512,512]{0,1:T(8,128)(4,1)} %broadcast_compare_fusion.6, ...), kind=kOutput, calls=%fused_computation.35.clone.1 | convolution fusion | flops 825360384 | bytes 18417152 | tf_op jit(solution)/shard_map/while/body/eval_jaxpr/bhqk,bkhd->bqhd/dot_general | solution.py:93
  665.7 7.7 fusion.214
  673.4 12.3 %bitcast_add_fusion.10 = f32[1,512,12,64]{1,3,2,0:T(8,128)} fusion(f32[1,512,12,64]{1,3,2,0:T(8,128)} %get-tuple-element.756, f32[12,512,512]{2,1,0:T(8,128)} %fusion.214, f32[12,512]{1,0:T(8,128)} %bitcast.358, f32[12,512]{1,0:T(8,128)} %bitcast.355, pred[512,512]{0,1:T(8,128)(4,1)} %broadcast_compare_fusion.6, ...), kind=kOutput, calls=%fused_computation.35.clone.1 | convolution fusion | flops 825360384 | bytes 18417152 | tf_op jit(solution)/shard_map/while/body/eval_jaxpr/bhqk,bkhd->bqhd/dot_general | solution.py:93
  686.6 7.7 fusion.214
  694.2 12.2 %bitcast_add_fusion.10 = f32[1,512,12,64]{1,3,2,0:T(8,128)} fusion(f32[1,512,12,64]{1,3,2,0:T(8,128)} %get-tuple-element.756, f32[12,512,512]{2,1,0:T(8,128)} %fusion.214, f32[12,512]{1,0:T(8,128)} %bitcast.358, f32[12,512]{1,0:T(8,128)} %bitcast.355, pred[512,512]{0,1:T(8,128)(4,1)} %broadcast_compare_fusion.6, ...), kind=kOutput, calls=%fused_computation.35.clone.1 | convolution fusion | flops 825360384 | bytes 18417152 | tf_op jit(solution)/shard_map/while/body/eval_jaxpr/bhqk,bkhd->bqhd/dot_general | solution.py:93
  707.3 7.7 fusion.214
  715.0 12.2 %bitcast_add_fusion.10 = f32[1,512,12,64]{1,3,2,0:T(8,128)} fusion(f32[1,512,12,64]{1,3,2,0:T(8,128)} %get-tuple-element.756, f32[12,512,512]{2,1,0:T(8,128)} %fusion.214, f32[12,512]{1,0:T(8,128)} %bitcast.358, f32[12,512]{1,0:T(8,128)} %bitcast.355, pred[512,512]{0,1:T(8,128)(4,1)} %broadcast_compare_fusion.6, ...), kind=kOutput, calls=%fused_computation.35.clone.1 | convolution fusion | flops 825360384 | bytes 18417152 | tf_op jit(solution)/shard_map/while/body/eval_jaxpr/bhqk,bkhd->bqhd/dot_general | solution.py:93
  728.1 7.7 fusion.214
  735.8 12.2 %bitcast_add_fusion.10 = f32[1,512,12,64]{1,3,2,0:T(8,128)} fusion(f32[1,512,12,64]{1,3,2,0:T(8,128)} %get-tuple-element.756, f32[12,512,512]{2,1,0:T(8,128)} %fusion.214, f32[12,512]{1,0:T(8,128)} %bitcast.358, f32[12,512]{1,0:T(8,128)} %bitcast.355, pred[512,512]{0,1:T(8,128)(4,1)} %broadcast_compare_fusion.6, ...), kind=kOutput, calls=%fused_computation.35.clone.1 | convolution fusion | flops 825360384 | bytes 18417152 | tf_op jit(solution)/shard_map/while/body/eval_jaxpr/bhqk,bkhd->bqhd/dot_general | solution.py:93
  749.0 8.6 fusion.214
  757.6 12.2 %bitcast_add_fusion.10 = f32[1,512,12,64]{1,3,2,0:T(8,128)} fusion(f32[1,512,12,64]{1,3,2,0:T(8,128)} %get-tuple-element.756, f32[12,512,512]{2,1,0:T(8,128)} %fusion.214, f32[12,512]{1,0:T(8,128)} %bitcast.358, f32[12,512]{1,0:T(8,128)} %bitcast.355, pred[512,512]{0,1:T(8,128)(4,1)} %broadcast_compare_fusion.6, ...), kind=kOutput, calls=%fused_computation.35.clone.1 | convolution fusion | flops 825360384 | bytes 18417152 | tf_op jit(solution)/shard_map/while/body/eval_jaxpr/bhqk,bkhd->bqhd/dot_general | solution.py:93
  770.7 7.7 fusion.214
  778.3 12.3 %bitcast_add_fusion.10 = f32[1,512,12,64]{1,3,2,0:T(8,128)} fusion(f32[1,512,12,64]{1,3,2,0:T(8,128)} %get-tuple-element.756, f32[12,512,512]{2,1,0:T(8,128)} %fusion.214, f32[12,512]{1,0:T(8,128)} %bitcast.358, f32[12,512]{1,0:T(8,128)} %bitcast.355, pred[512,512]{0,1:T(8,128)(4,1)} %broadcast_compare_fusion.6, ...), kind=kOutput, calls=%fused_computation.35.clone.1 | convolution fusion | flops 825360384 | bytes 18417152 | tf_op jit(solution)/shard_map/while/body/eval_jaxpr/bhqk,bkhd->bqhd/dot_general | solution.py:93
  796.4 6.7 fusion.122
  815.8 38.5 %reduce-scatter.14.cloned.1.call-done = bf16[1,384,768]{2,1,0:T(8,128)(2,1)} async-done(((bf16[1,3072,768]{2,1,0:T(8,128)(2,1)}), bf16[1,384,768]{2,1,0:T(8,128)(2,1)}) %reduce-scatter.14.cloned.1.call-update) | async-done | bytes 589840 | tf_op jit(solution)/shard_map/reduce_scatter | solution.py:336
  864.6 42.6 %all-reduce = (f32[768]{0:T(1024)}, f32[768]{0:T(1024)}, f32[768]{0:T(1024)}, f32[768]{0:T(1024)}, f32[768]{0:T(1024)}, /*index=5*/f32[768]{0:T(1024)}, f32[768]{0:T(1024)}) all-reduce(f32[768]{0:T(1024)} %get-tuple-element.487, f32[768]{0:T(1024)} %get-tuple-element.491, ...), channel_id=1, replica_groups=mesh['seq'=8,'exp'=4] {'seq','exp'}, use_global_device_ids=true, to_apply=%region_24.26 | all-reduce | flops 5376 | bytes 43008 | tf_op jit(solution)/shard_map/psum | solution.py:343
  912.1 142.1 %all-reduce.4.cloned.1.call-done = (f32[768,2304]{1,0:T(8,128)}, f32[768,768]{1,0:T(8,128)}) async-done(((f32[768,2304]{1,0:T(8,128)}, f32[768,768]{1,0:T(8,128)}), (f32[768,2304]{1,0:T(8,128)}, f32[768,768]{1,0:T(8,128)})) %all-reduce.4.cloned.1.call-update) | async-done | bytes 9437200 | tf_op jit(solution)/shard_map/psum | solution.py:343
  1054.2 6.6 copy.110
  (357 shorter events, 305.7 us)
Async XLA Ops:
  7.2 423.4 %all-gather.3.cloned.1.call-start = ((), (), s32[]{:S(2)}) async-start(), calls=%async_computation.9 | async-start | bytes 7077888 | tf_op jit(solution)/shard_map/all_gather | solution.py:281
  55.2 20.3 %collective-permute-start = (bf16[1,512,12,64]{1,3,2,0:T(8,128)(2,1)}, bf16[1,512,12,64]{1,3,2,0:T(8,128)(2,1)}, u32[]{:S(2)}, u32[]{:S(2)}) collective-permute-start(bf16[1,512,12,64]{1,3,2,0:T(8,128)(2,1)} %get-tuple-element.715), channel_id=1, source_target_pairs={{28,0},{0,4},{4,8},{8,12},{12,16},{16,20},{20,24},{24,28},{29,1},{... | collective-permute-start | bytes 2359304 | tf_op jit(solution)/shard_map/while/body/eval_jaxpr/ppermute | solution.py:28
  57.1 21.9 %collective-permute-start.1 = (bf16[1,12,512]{2,1,0:T(8,128)(2,1)}, bf16[1,12,512]{2,1,0:T(8,128)(2,1)S(1)}, u32[]{:S(2)}, u32[]{:S(2)}) collective-permute-start(bf16[1,12,512]{2,1,0:T(8,128)(2,1)} %convert_element_type.427), channel_id=1, source_target_pairs={{28,0},{0,4},{4,8},{8,12},{12,16},{16,20},{20,24},{24,28},{29,1},{... | collective-permute-start | bytes 36872 | tf_op jit(solution)/shard_map/while/body/eval_jaxpr/ppermute | solution.py:28
  59.9 24.7 %collective-permute-start.2 = (bf16[1,12,512]{2,1,0:T(8,128)(2,1)}, bf16[1,12,512]{2,1,0:T(8,128)(2,1)}, u32[]{:S(2)}, u32[]{:S(2)}) collective-permute-start(bf16[1,12,512]{2,1,0:T(8,128)(2,1)} %get-tuple-element.717), channel_id=1, source_target_pairs={{28,0},{0,4},{4,8},{8,12},{12,16},{16,20},{20,24},{24,28},{29,1},{... | collective-permute-start | bytes 36872 | tf_op jit(solution)/shard_map/while/body/eval_jaxpr/ppermute | solution.py:28
  59.9 26.0 %collective-permute-start.3 = (bf16[1,512,12,64]{1,3,2,0:T(8,128)(2,1)}, bf16[1,512,12,64]{1,3,2,0:T(8,128)(2,1)}, u32[]{:S(2)}, u32[]{:S(2)}) collective-permute-start(bf16[1,512,12,64]{1,3,2,0:T(8,128)(2,1)} %get-tuple-element.718), channel_id=1, source_target_pairs={{28,0},{0,4},{4,8},{8,12},{12,16},{16,20},{20,24},{24,28},{29,1},{... | collective-permute-start | bytes 2359304 | tf_op jit(solution)/shard_map/while/body/eval_jaxpr/ppermute | solution.py:28
  91.4 12.6 %collective-permute-start = (bf16[1,512,12,64]{1,3,2,0:T(8,128)(2,1)}, bf16[1,512,12,64]{1,3,2,0:T(8,128)(2,1)}, u32[]{:S(2)}, u32[]{:S(2)}) collective-permute-start(bf16[1,512,12,64]{1,3,2,0:T(8,128)(2,1)} %get-tuple-element.715), channel_id=1, source_target_pairs={{28,0},{0,4},{4,8},{8,12},{12,16},{16,20},{20,24},{24,28},{29,1},{... | collective-permute-start | bytes 2359304 | tf_op jit(solution)/shard_map/while/body/eval_jaxpr/ppermute | solution.py:28
  92.8 14.7 %collective-permute-start.1 = (bf16[1,12,512]{2,1,0:T(8,128)(2,1)}, bf16[1,12,512]{2,1,0:T(8,128)(2,1)S(1)}, u32[]{:S(2)}, u32[]{:S(2)}) collective-permute-start(bf16[1,12,512]{2,1,0:T(8,128)(2,1)} %convert_element_type.427), channel_id=1, source_target_pairs={{28,0},{0,4},{4,8},{8,12},{12,16},{16,20},{20,24},{24,28},{29,1},{... | collective-permute-start | bytes 36872 | tf_op jit(solution)/shard_map/while/body/eval_jaxpr/ppermute | solution.py:28
  92.8 20.4 %collective-permute-start.2 = (bf16[1,12,512]{2,1,0:T(8,128)(2,1)}, bf16[1,12,512]{2,1,0:T(8,128)(2,1)}, u32[]{:S(2)}, u32[]{:S(2)}) collective-permute-start(bf16[1,12,512]{2,1,0:T(8,128)(2,1)} %get-tuple-element.717), channel_id=1, source_target_pairs={{28,0},{0,4},{4,8},{8,12},{12,16},{16,20},{20,24},{24,28},{29,1},{... | collective-permute-start | bytes 36872 | tf_op jit(solution)/shard_map/while/body/eval_jaxpr/ppermute | solution.py:28
  92.8 21.7 %collective-permute-start.3 = (bf16[1,512,12,64]{1,3,2,0:T(8,128)(2,1)}, bf16[1,512,12,64]{1,3,2,0:T(8,128)(2,1)}, u32[]{:S(2)}, u32[]{:S(2)}) collective-permute-start(bf16[1,512,12,64]{1,3,2,0:T(8,128)(2,1)} %get-tuple-element.718), channel_id=1, source_target_pairs={{28,0},{0,4},{4,8},{8,12},{12,16},{16,20},{20,24},{24,28},{29,1},{... | collective-permute-start | bytes 2359304 | tf_op jit(solution)/shard_map/while/body/eval_jaxpr/ppermute | solution.py:28
  119.9 12.6 %collective-permute-start = (bf16[1,512,12,64]{1,3,2,0:T(8,128)(2,1)}, bf16[1,512,12,64]{1,3,2,0:T(8,128)(2,1)}, u32[]{:S(2)}, u32[]{:S(2)}) collective-permute-start(bf16[1,512,12,64]{1,3,2,0:T(8,128)(2,1)} %get-tuple-element.715), channel_id=1, source_target_pairs={{28,0},{0,4},{4,8},{8,12},{12,16},{16,20},{20,24},{24,28},{29,1},{... | collective-permute-start | bytes 2359304 | tf_op jit(solution)/shard_map/while/body/eval_jaxpr/ppermute | solution.py:28
  121.2 14.7 %collective-permute-start.1 = (bf16[1,12,512]{2,1,0:T(8,128)(2,1)}, bf16[1,12,512]{2,1,0:T(8,128)(2,1)S(1)}, u32[]{:S(2)}, u32[]{:S(2)}) collective-permute-start(bf16[1,12,512]{2,1,0:T(8,128)(2,1)} %convert_element_type.427), channel_id=1, source_target_pairs={{28,0},{0,4},{4,8},{8,12},{12,16},{16,20},{20,24},{24,28},{29,1},{... | collective-permute-start | bytes 36872 | tf_op jit(solution)/shard_map/while/body/eval_jaxpr/ppermute | solution.py:28
  121.2 20.4 %collective-permute-start.2 = (bf16[1,12,512]{2,1,0:T(8,128)(2,1)}, bf16[1,12,512]{2,1,0:T(8,128)(2,1)}, u32[]{:S(2)}, u32[]{:S(2)}) collective-permute-start(bf16[1,12,512]{2,1,0:T(8,128)(2,1)} %get-tuple-element.717), channel_id=1, source_target_pairs={{28,0},{0,4},{4,8},{8,12},{12,16},{16,20},{20,24},{24,28},{29,1},{... | collective-permute-start | bytes 36872 | tf_op jit(solution)/shard_map/while/body/eval_jaxpr/ppermute | solution.py:28
  121.2 21.7 %collective-permute-start.3 = (bf16[1,512,12,64]{1,3,2,0:T(8,128)(2,1)}, bf16[1,512,12,64]{1,3,2,0:T(8,128)(2,1)}, u32[]{:S(2)}, u32[]{:S(2)}) collective-permute-start(bf16[1,512,12,64]{1,3,2,0:T(8,128)(2,1)} %get-tuple-element.718), channel_id=1, source_target_pairs={{28,0},{0,4},{4,8},{8,12},{12,16},{16,20},{20,24},{24,28},{29,1},{... | collective-permute-start | bytes 2359304 | tf_op jit(solution)/shard_map/while/body/eval_jaxpr/ppermute | solution.py:28
  148.4 12.6 %collective-permute-start = (bf16[1,512,12,64]{1,3,2,0:T(8,128)(2,1)}, bf16[1,512,12,64]{1,3,2,0:T(8,128)(2,1)}, u32[]{:S(2)}, u32[]{:S(2)}) collective-permute-start(bf16[1,512,12,64]{1,3,2,0:T(8,128)(2,1)} %get-tuple-element.715), channel_id=1, source_target_pairs={{28,0},{0,4},{4,8},{8,12},{12,16},{16,20},{20,24},{24,28},{29,1},{... | collective-permute-start | bytes 2359304 | tf_op jit(solution)/shard_map/while/body/eval_jaxpr/ppermute | solution.py:28
  149.7 14.7 %collective-permute-start.1 = (bf16[1,12,512]{2,1,0:T(8,128)(2,1)}, bf16[1,12,512]{2,1,0:T(8,128)(2,1)S(1)}, u32[]{:S(2)}, u32[]{:S(2)}) collective-permute-start(bf16[1,12,512]{2,1,0:T(8,128)(2,1)} %convert_element_type.427), channel_id=1, source_target_pairs={{28,0},{0,4},{4,8},{8,12},{12,16},{16,20},{20,24},{24,28},{29,1},{... | collective-permute-start | bytes 36872 | tf_op jit(solution)/shard_map/while/body/eval_jaxpr/ppermute | solution.py:28
  149.7 20.4 %collective-permute-start.2 = (bf16[1,12,512]{2,1,0:T(8,128)(2,1)}, bf16[1,12,512]{2,1,0:T(8,128)(2,1)}, u32[]{:S(2)}, u32[]{:S(2)}) collective-permute-start(bf16[1,12,512]{2,1,0:T(8,128)(2,1)} %get-tuple-element.717), channel_id=1, source_target_pairs={{28,0},{0,4},{4,8},{8,12},{12,16},{16,20},{20,24},{24,28},{29,1},{... | collective-permute-start | bytes 36872 | tf_op jit(solution)/shard_map/while/body/eval_jaxpr/ppermute | solution.py:28
  149.7 21.7 %collective-permute-start.3 = (bf16[1,512,12,64]{1,3,2,0:T(8,128)(2,1)}, bf16[1,512,12,64]{1,3,2,0:T(8,128)(2,1)}, u32[]{:S(2)}, u32[]{:S(2)}) collective-permute-start(bf16[1,512,12,64]{1,3,2,0:T(8,128)(2,1)} %get-tuple-element.718), channel_id=1, source_target_pairs={{28,0},{0,4},{4,8},{8,12},{12,16},{16,20},{20,24},{24,28},{29,1},{... | collective-permute-start | bytes 2359304 | tf_op jit(solution)/shard_map/while/body/eval_jaxpr/ppermute | solution.py:28
  176.8 12.6 %collective-permute-start = (bf16[1,512,12,64]{1,3,2,0:T(8,128)(2,1)}, bf16[1,512,12,64]{1,3,2,0:T(8,128)(2,1)}, u32[]{:S(2)}, u32[]{:S(2)}) collective-permute-start(bf16[1,512,12,64]{1,3,2,0:T(8,128)(2,1)} %get-tuple-element.715), channel_id=1, source_target_pairs={{28,0},{0,4},{4,8},{8,12},{12,16},{16,20},{20,24},{24,28},{29,1},{... | collective-permute-start | bytes 2359304 | tf_op jit(solution)/shard_map/while/body/eval_jaxpr/ppermute | solution.py:28
  178.2 14.7 %collective-permute-start.1 = (bf16[1,12,512]{2,1,0:T(8,128)(2,1)}, bf16[1,12,512]{2,1,0:T(8,128)(2,1)S(1)}, u32[]{:S(2)}, u32[]{:S(2)}) collective-permute-start(bf16[1,12,512]{2,1,0:T(8,128)(2,1)} %convert_element_type.427), channel_id=1, source_target_pairs={{28,0},{0,4},{4,8},{8,12},{12,16},{16,20},{20,24},{24,28},{29,1},{... | collective-permute-start | bytes 36872 | tf_op jit(solution)/shard_map/while/body/eval_jaxpr/ppermute | solution.py:28
  178.2 20.4 %collective-permute-start.2 = (bf16[1,12,512]{2,1,0:T(8,128)(2,1)}, bf16[1,12,512]{2,1,0:T(8,128)(2,1)}, u32[]{:S(2)}, u32[]{:S(2)}) collective-permute-start(bf16[1,12,512]{2,1,0:T(8,128)(2,1)} %get-tuple-element.717), channel_id=1, source_target_pairs={{28,0},{0,4},{4,8},{8,12},{12,16},{16,20},{20,24},{24,28},{29,1},{... | collective-permute-start | bytes 36872 | tf_op jit(solution)/shard_map/while/body/eval_jaxpr/ppermute | solution.py:28
  178.2 21.7 %collective-permute-start.3 = (bf16[1,512,12,64]{1,3,2,0:T(8,128)(2,1)}, bf16[1,512,12,64]{1,3,2,0:T(8,128)(2,1)}, u32[]{:S(2)}, u32[]{:S(2)}) collective-permute-start(bf16[1,512,12,64]{1,3,2,0:T(8,128)(2,1)} %get-tuple-element.718), channel_id=1, source_target_pairs={{28,0},{0,4},{4,8},{8,12},{12,16},{16,20},{20,24},{24,28},{29,1},{... | collective-permute-start | bytes 2359304 | tf_op jit(solution)/shard_map/while/body/eval_jaxpr/ppermute | solution.py:28
  205.3 12.6 %collective-permute-start = (bf16[1,512,12,64]{1,3,2,0:T(8,128)(2,1)}, bf16[1,512,12,64]{1,3,2,0:T(8,128)(2,1)}, u32[]{:S(2)}, u32[]{:S(2)}) collective-permute-start(bf16[1,512,12,64]{1,3,2,0:T(8,128)(2,1)} %get-tuple-element.715), channel_id=1, source_target_pairs={{28,0},{0,4},{4,8},{8,12},{12,16},{16,20},{20,24},{24,28},{29,1},{... | collective-permute-start | bytes 2359304 | tf_op jit(solution)/shard_map/while/body/eval_jaxpr/ppermute | solution.py:28
  206.7 14.7 %collective-permute-start.1 = (bf16[1,12,512]{2,1,0:T(8,128)(2,1)}, bf16[1,12,512]{2,1,0:T(8,128)(2,1)S(1)}, u32[]{:S(2)}, u32[]{:S(2)}) collective-permute-start(bf16[1,12,512]{2,1,0:T(8,128)(2,1)} %convert_element_type.427), channel_id=1, source_target_pairs={{28,0},{0,4},{4,8},{8,12},{12,16},{16,20},{20,24},{24,28},{29,1},{... | collective-permute-start | bytes 36872 | tf_op jit(solution)/shard_map/while/body/eval_jaxpr/ppermute | solution.py:28
  206.7 20.4 %collective-permute-start.2 = (bf16[1,12,512]{2,1,0:T(8,128)(2,1)}, bf16[1,12,512]{2,1,0:T(8,128)(2,1)}, u32[]{:S(2)}, u32[]{:S(2)}) collective-permute-start(bf16[1,12,512]{2,1,0:T(8,128)(2,1)} %get-tuple-element.717), channel_id=1, source_target_pairs={{28,0},{0,4},{4,8},{8,12},{12,16},{16,20},{20,24},{24,28},{29,1},{... | collective-permute-start | bytes 36872 | tf_op jit(solution)/shard_map/while/body/eval_jaxpr/ppermute | solution.py:28
  206.7 21.7 %collective-permute-start.3 = (bf16[1,512,12,64]{1,3,2,0:T(8,128)(2,1)}, bf16[1,512,12,64]{1,3,2,0:T(8,128)(2,1)}, u32[]{:S(2)}, u32[]{:S(2)}) collective-permute-start(bf16[1,512,12,64]{1,3,2,0:T(8,128)(2,1)} %get-tuple-element.718), channel_id=1, source_target_pairs={{28,0},{0,4},{4,8},{8,12},{12,16},{16,20},{20,24},{24,28},{29,1},{... | collective-permute-start | bytes 2359304 | tf_op jit(solution)/shard_map/while/body/eval_jaxpr/ppermute | solution.py:28
  233.8 12.6 %collective-permute-start = (bf16[1,512,12,64]{1,3,2,0:T(8,128)(2,1)}, bf16[1,512,12,64]{1,3,2,0:T(8,128)(2,1)}, u32[]{:S(2)}, u32[]{:S(2)}) collective-permute-start(bf16[1,512,12,64]{1,3,2,0:T(8,128)(2,1)} %get-tuple-element.715), channel_id=1, source_target_pairs={{28,0},{0,4},{4,8},{8,12},{12,16},{16,20},{20,24},{24,28},{29,1},{... | collective-permute-start | bytes 2359304 | tf_op jit(solution)/shard_map/while/body/eval_jaxpr/ppermute | solution.py:28
  235.2 14.7 %collective-permute-start.1 = (bf16[1,12,512]{2,1,0:T(8,128)(2,1)}, bf16[1,12,512]{2,1,0:T(8,128)(2,1)S(1)}, u32[]{:S(2)}, u32[]{:S(2)}) collective-permute-start(bf16[1,12,512]{2,1,0:T(8,128)(2,1)} %convert_element_type.427), channel_id=1, source_target_pairs={{28,0},{0,4},{4,8},{8,12},{12,16},{16,20},{20,24},{24,28},{29,1},{... | collective-permute-start | bytes 36872 | tf_op jit(solution)/shard_map/while/body/eval_jaxpr/ppermute | solution.py:28
  235.2 20.4 %collective-permute-start.2 = (bf16[1,12,512]{2,1,0:T(8,128)(2,1)}, bf16[1,12,512]{2,1,0:T(8,128)(2,1)}, u32[]{:S(2)}, u32[]{:S(2)}) collective-permute-start(bf16[1,12,512]{2,1,0:T(8,128)(2,1)} %get-tuple-element.717), channel_id=1, source_target_pairs={{28,0},{0,4},{4,8},{8,12},{12,16},{16,20},{20,24},{24,28},{29,1},{... | collective-permute-start | bytes 36872 | tf_op jit(solution)/shard_map/while/body/eval_jaxpr/ppermute | solution.py:28
  235.2 21.7 %collective-permute-start.3 = (bf16[1,512,12,64]{1,3,2,0:T(8,128)(2,1)}, bf16[1,512,12,64]{1,3,2,0:T(8,128)(2,1)}, u32[]{:S(2)}, u32[]{:S(2)}) collective-permute-start(bf16[1,512,12,64]{1,3,2,0:T(8,128)(2,1)} %get-tuple-element.718), channel_id=1, source_target_pairs={{28,0},{0,4},{4,8},{8,12},{12,16},{16,20},{20,24},{24,28},{29,1},{... | collective-permute-start | bytes 2359304 | tf_op jit(solution)/shard_map/while/body/eval_jaxpr/ppermute | solution.py:28
  262.3 17.0 %collective-permute-start.5 = (bf16[1,12,512]{2,1,0:T(8,128)(2,1)}, bf16[1,12,512]{2,1,0:T(8,128)(2,1)}, u32[]{:S(2)}, u32[]{:S(2)}) collective-permute-start(bf16[1,12,512]{2,1,0:T(8,128)(2,1)} %get-tuple-element.436), channel_id=1, source_target_pairs={{28,0},{0,4},{4,8},{8,12},{12,16},{16,20},{20,24},{24,28},{29,1},{... | collective-permute-start | bytes 36872 | tf_op jit(solution)/shard_map/ppermute | solution.py:28
  262.3 17.8 %collective-permute-start.4 = (bf16[1,512,12,64]{1,3,2,0:T(8,128)(2,1)}, bf16[1,512,12,64]{1,3,2,0:T(8,128)(2,1)}, u32[]{:S(2)}, u32[]{:S(2)}) collective-permute-start(bf16[1,512,12,64]{1,3,2,0:T(8,128)(2,1)} %get-tuple-element.435), channel_id=1, source_target_pairs={{28,0},{0,4},{4,8},{8,12},{12,16},{16,20},{20,24},{24,28},{29,1},{... | collective-permute-start | bytes 2359304 | tf_op jit(solution)/shard_map/ppermute | solution.py:28
  266.8 18.8 %copy-start.19 = (f32[768]{0:T(1024)S(1)}, f32[768]{0:T(1024)}, u32[]{:S(2)}) copy-start(f32[768]{0:T(1024)} %param.35) | copy-start | bytes 9220
  285.5 59.9 %copy-start.30 = (f32[512]{0:T(512)}, f32[512]{0:T(512)S(1)}, u32[]{:S(2)}) copy-start(f32[512]{0:T(512)S(1)} %multiply_reduce_fusion.3) | copy-start | bytes 6148
  290.3 28.0 %all-to-all-start = ((bf16[4,1,160,768]{3,2,1,0:T(8,128)(2,1)}), bf16[4,1,160,768]{3,2,1,0:T(8,128)(2,1)}, u32[]{:S(2)}, u32[]{:S(2)}) async-start(bf16[4,1,160,768]{3,2,1,0:T(8,128)(2,1)} %bitcast.335), calls=%async_computation | async-start | bytes 1966080 | tf_op jit(solution)/shard_map/all_to_all | solution.py:243
  294.9 212.8 %all-gather.5.cloned.1.call-start = ((), (), s32[]{:S(2)}) async-start(), calls=%async_computation.10 | async-start | bytes 7077888 | tf_op jit(solution)/shard_map/all_gather | solution.py:282
  297.0 94.2 %collective-permute-start.6 = (bf16[1,12,512]{2,1,0:T(8,128)(2,1)}, bf16[1,12,512]{2,1,0:T(8,128)(2,1)}, u32[]{:S(2)}, u32[]{:S(2)}) collective-permute-start(bf16[1,12,512]{2,1,0:T(8,128)(2,1)} %convert_element_type.256), channel_id=1, source_target_pairs={{28,0},{0,4},{4,8},{8,12},{12,16},{16,20},{20,24},{24,28},{29,1},{... | collective-permute-start | bytes 36872 | tf_op jit(solution)/shard_map/ppermute | solution.py:28
  318.3 35.5 %all-to-all-start.2 = ((bf16[4,1,160,768]{3,2,1,0:T(8,128)(2,1)}), bf16[4,1,160,768]{3,2,1,0:T(8,128)(2,1)}, u32[]{:S(2)}, u32[]{:S(2)}) async-start(bf16[4,1,160,768]{3,2,1,0:T(8,128)(2,1)} %bitcast.336), calls=%async_computation.2 | async-start | bytes 1966080 | tf_op jit(solution)/shard_map/all_to_all | solution.py:257
  322.8 24.5 %copy-start.40 = (f32[768]{0:T(1024)S(1)}, f32[768]{0:T(1024)}, u32[]{:S(2)}) copy-start(f32[768]{0:T(1024)} %reduce.27) | copy-start | bytes 9220
  353.8 28.4 %all-to-all-start.1 = ((bf16[1,4,160,768]{3,2,0,1:T(8,128)(2,1)}), bf16[1,4,160,768]{3,2,0,1:T(8,128)(2,1)}, u32[]{:S(2)}, u32[]{:S(2)}) async-start(bf16[1,4,160,768]{3,2,0,1:T(8,128)(2,1)} %bitcast.349), calls=%async_computation.1 | async-start | bytes 1966080 | tf_op jit(solution)/shard_map/all_to_all | solution.py:245
  382.3 28.1 %all-to-all-start.3 = ((bf16[1,4,160,768]{3,2,0,1:T(8,128)(2,1)}), bf16[1,4,160,768]{3,2,0,1:T(8,128)(2,1)}, u32[]{:S(2)}, u32[]{:S(2)}) async-start(bf16[1,4,160,768]{3,2,0,1:T(8,128)(2,1)} %bitcast.348), calls=%async_computation.3 | async-start | bytes 1966080 | tf_op jit(solution)/shard_map/all_to_all | solution.py:261
  386.5 407.2 %reduce-scatter.12.cloned.1.call-start = ((), (), s32[]{:S(2)}) async-start(), calls=%async_computation.11 | async-start | bytes 14155776 | tf_op jit(solution)/shard_map/reduce_scatter | solution.py:300
  391.2 19.2 %copy-start.36 = (s32[1024]{0:T(1024)}, s32[1024]{0:T(1024)S(1)}, u32[]{:S(2)}) copy-start(s32[1024]{0:T(1024)S(1)} %pad_clamp_fusion) | copy-start | bytes 12292
  570.1 233.0 %reduce-scatter.20.cloned.1.call-start = ((), (), s32[]{:S(2)}) async-start(), calls=%async_computation.15 | async-start | bytes 221184
  572.4 232.1 %reduce-scatter.18.cloned.1.call-start = ((), (), s32[]{:S(2)}) async-start(), calls=%async_computation.14 | async-start | bytes 884736
  573.9 232.2 %reduce-scatter.16.cloned.1.call-start = ((), (), s32[]{:S(2)}) async-start(), calls=%async_computation.13 | async-start | bytes 5308416
  610.7 243.6 %reduce-scatter.14.cloned.1.call-start = ((), (), s32[]{:S(2)}) async-start(), calls=%async_computation.12 | async-start | bytes 5308416 | tf_op jit(solution)/shard_map/reduce_scatter | solution.py:336
  619.5 434.7 %all-reduce.4.cloned.1.call-start = ((), (), s32[]{:S(2)}) async-start(), calls=%async_computation.16 | async-start | bytes 18874368 | tf_op jit(solution)/shard_map/psum | solution.py:343
  858.4 49.4 %copy-start.27 = (f32[512]{0:T(512)S(1)}, f32[512]{0:T(512)}, u32[]{:S(2)}) copy-start(f32[512]{0:T(512)} %copy-done.26) | copy-start | bytes 6148
  (52 other events, 314.1 us)
Sparse Core Ops, SparseCore 0:
  19.8 52.3 all-gather.2
  297.6 48.7 all-gather.4
  570.3 93.6 reduce-scatter.11
  666.9 33.5 reduce-scatter.19
  704.3 34.9 reduce-scatter.17
  743.0 53.9 reduce-scatter.15
  800.4 53.8 reduce-scatter.13
  861.9 192.2 all-reduce.3
where the time goes:
time: 1080 us; the launch traced here: 1070 us
  matrix products  450 us (42%)
  waiting for transfers between devices  283 us (26%)
  other arithmetic  134 us (12%)
  local copies, waits for them, and re-layouts  107 us (10%)
  blocking collectives  42.6 us (4%)
  starting transfers between devices  37.9 us (4%)
  between operations  15.1 us (1%)
    psum x1, waiting for transfers between devices, local(): lax.psum((grad_ln1_gain, grad_ln1_bias, grad_w_qkv, grad_q_bias, grad_v_b...  142 us
    dot_general x17, matrix products, scores_at(): jnp.einsum('bqhd,bkhd->bhqk', queries, keys_part, preferred_element_type=...  132 us
    dot_general x8, matrix products, grads_at(): jnp.einsum('bhqk,bkhd->bqhd', grad_scores, keys_part, preferred_element_t...  97.3 us
    ppermute x31, waiting for transfers between devices, passed_along(): return lax.ppermute(block, axis, route)  66.5 us
    unnamed x97, local copies, waits for them, and re-layouts  61.7 us
    dot_general x1, matrix products, grads_at(): jnp.einsum('bhqk,bqhd->bkhd', grad_scores, queries, preferred_element_typ...  52 us
    dot_general x8, matrix products, attend_block(): jnp.einsum('bhqk,bkhd->bqhd', weights.astype(jnp.bfloat16), values_part,...  43.6 us
    psum x1, blocking collectives, local(): lax.psum((grad_ln1_gain, grad_ln1_bias, grad_w_qkv, grad_q_bias, grad_v_b...  42.6 us
  transfers between devices with their start and end apart: 43, of which 12 were waited for; matrix products, arithmetic and copies ran while one was open for 56% of the time, Pallas kernels for 0%

commit v1 on v0

v1 whole, which is shorter than its diff:
```python
from functools import partial
import math

import jax
import jax.numpy as jnp
from jax import lax
from jax.experimental import pallas as pl
from jax.experimental.pallas import tpu as pltpu
from jax.sharding import PartitionSpec as P

HEADS = 12
HEAD_DIM = 64
f32 = jnp.float32
bf16 = jnp.bfloat16

norm_eps = 1e-05
logit_scale = 0.125
masked_score = -1e30
LOG2E = math.log2(math.e)

QT = 512
KC = 1024
SUB = 256
VMEM = 56 * 2**20


def rows_of(start, size):
    return pl.ds(pl.multiple_of(start, size), size)


def fwd_kernel(
    n_ref,
    base_ref,
    tile_ref,
    q_ref,
    k_ref,
    vt_ref,
    place_ref,
    o_ref,
    linv_ref,
    p_hbm,
    s_scr,
    p_scr,
    m_scr,
    acc_scr,
    l_scr,
    sem,
):
    i = pl.program_id(0)
    last = pl.num_programs(0) - 1
    a = lax.rem(i, 2)
    b = 1 - a
    before = jnp.maximum(i - 1, 0)
    n1 = n_ref[i]
    n2 = n_ref[before]
    base1 = base_ref[i]
    base2 = base_ref[before]

    def first(c, masked):
        q = q_ref[...]
        m = m_scr[a]
        for j in range(KC // SUB):
            off = c * KC + j * SUB
            s = jnp.dot(k_ref[rows_of(base1 + off, SUB), :], q, preferred_element_type=f32)
            if masked:
                key = lax.broadcasted_iota(jnp.int32, (SUB, QT), 0)
                s = jnp.where(key <= place_ref[...] - off, s, masked_score)
            s_scr[a, rows_of(off, SUB), :] = s
            m = jnp.maximum(m, jnp.max(s.reshape(SUB // 8, 8, QT), axis=0))
        m_scr[a] = m

    def second(c):
        top = jnp.max(m_scr[b], axis=0, keepdims=True) * (logit_scale * LOG2E)
        l = l_scr[...]
        for j in range(KC // SUB):
            off = c * KC + j * SUB
            s = s_scr[b, rows_of(off, SUB), :]
            p = jnp.exp2(s * (logit_scale * LOG2E) - top)
            l = l + jnp.sum(p.reshape(SUB // 8, 8, QT), axis=0)
            low = p.astype(bf16)
            p_scr[b, rows_of(off, SUB), :] = low
            acc_scr[...] += jnp.dot(
                vt_ref[:, rows_of(base2 + off, SUB)], low, preferred_element_type=f32
            )
        l_scr[...] = l
        part = rows_of(c * KC, KC)
        pltpu.make_async_copy(p_scr.at[b, part], p_hbm.at[before, part], sem.at[b]).start()

    def drain(count, slot):
        def wait(c, _):
            part = pl.ds(0, KC)
            pltpu.make_async_copy(p_scr.at[slot, part], p_hbm.at[0, part], sem.at[slot]).wait()
            return 0

        lax.fori_loop(0, count, wait, 0)

    def loop(low, high, do):
        def step(c, _):
            do(c)
            return 0

        lax.fori_loop(low, high, step, 0)

    m_scr[a] = jnp.full((8, QT), -jnp.inf, f32)

    @pl.when(i >= 1)
    def _():
        l_scr[...] = jnp.zeros_like(l_scr)
        acc_scr[...] = jnp.zeros_like(acc_scr)

    @pl.when(i >= 3)
    def _():
        drain(n_ref[jnp.maximum(i - 3, 0)], b)

    @pl.when(i == 0)
    def _():
        loop(0, n1, lambda c: first(c, True))

    @pl.when(jnp.logical_and(i > 0, i < last))
    def _():
        first(n1 - 1, True)
        second(n2 - 1)
        both = jnp.minimum(n1, n2) - 1

        def step(c):
            first(c, False)
            second(c)

        loop(0, both, step)
        loop(both, n1 - 1, lambda c: first(c, False))
        loop(both, n2 - 1, second)

    @pl.when(i == last)
    def _():
        loop(0, n2, second)

    @pl.when(i > 0)
    def _():
        linv = 1.0 / jnp.sum(l_scr[...], axis=0, keepdims=True)
        o_ref[...] = acc_scr[...] * linv
        linv_ref[...] = linv

    @pl.when(i == last)
    def _():
        drain(n_ref[jnp.maximum(i - 2, 0)], a)
        drain(n2, b)


def tile_lists(tiles, nk):
    final = (tiles[-1][0], tiles[-1][1], 0)
    parity = [0]
    for t in tiles:
        parity.append((parity[-1] + t[2]) % 2)
    listed = tiles + [final]
    return (
        jnp.array([t[2] for t in listed], jnp.int32),
        jnp.array([t[1] * nk for t in listed], jnp.int32),
        jnp.array([t[0] for t in listed], jnp.int32),
        jnp.array(parity, jnp.int32),
    )


def pair_units(tiles):
    return sum(t[2] for t in tiles) * KC * QT


def attn_fwd(qt, k, vt, place, tiles, nk):
    count, base, which, _ = tile_lists(tiles, nk)
    nq = qt.shape[1]
    steps = len(tiles)

    def now(r):
        return pl.BlockSpec((r, QT), lambda i, n, b, s: (0, s[i]))

    def prev(r):
        return pl.BlockSpec((r, QT), lambda i, n, b, s: (0, s[jnp.maximum(i - 1, 0)]))

    def whole(x):
        return pl.BlockSpec(x.shape, lambda i, n, b, s: (0, 0))

    work = pair_units(tiles)
    return pl.pallas_call(
        fwd_kernel,
        name="attn_fwd",
        grid_spec=pltpu.PrefetchScalarGridSpec(
            num_scalar_prefetch=3,
            grid=(steps + 1,),
            in_specs=[now(HEAD_DIM), whole(k), whole(vt), now(1)],
            out_specs=[prev(HEAD_DIM), prev(1), pl.BlockSpec(memory_space=pl.ANY)],
            scratch_shapes=[
                pltpu.VMEM((2, nk, QT), f32),
                pltpu.VMEM((2, nk, QT), bf16),
                pltpu.VMEM((2, 8, QT), f32),
                pltpu.VMEM((HEAD_DIM, QT), f32),
                pltpu.VMEM((8, QT), f32),
                pltpu.SemaphoreType.DMA((2,)),
            ],
        ),
        out_shape=[
            jax.ShapeDtypeStruct((HEAD_DIM, nq), f32),
            jax.ShapeDtypeStruct((1, nq), f32),
            jax.ShapeDtypeStruct((steps, nk, QT), bf16),
        ],
        compiler_params=pltpu.CompilerParams(vmem_limit_bytes=VMEM),
        cost_estimate=pl.CostEstimate(
            flops=work * 1024, bytes_accessed=work * 2, transcendentals=work
        ),
    )(count, base, which, qt, k, vt, place)


def bwd_kernel(
    n_ref,
    base_ref,
    tile_ref,
    parity_ref,
    qt_ref,
    dot_ref,
    o_ref,
    linv_ref,
    kt_ref,
    v_ref,
    p_hbm,
    dq_ref,
    dk_ref,
    dv_ref,
    p_scr,
    dp_scr,
    q_scr,
    do_scr,
    de_scr,
    dq_scr,
    sem,
):
    i = pl.program_id(0)
    last = pl.num_programs(0) - 1
    a = lax.rem(i, 2)
    b = 1 - a
    before = jnp.maximum(i - 1, 0)
    n1 = n_ref[i]
    n2 = n_ref[before]
    base1 = base_ref[i]
    base2 = base_ref[before]
    par1 = parity_ref[i]
    par2 = parity_ref[before]

    def fetch(t, slot):
        def start(c, _):
            part = rows_of(c * KC, KC)
            pltpu.make_async_copy(p_hbm.at[t, part], p_scr.at[slot, part], sem.at[slot]).start()
            return 0

        lax.fori_loop(0, n_ref[t], start, 0)

    def dp_of(c):
        for j in range(KC // SUB):
            off = c * KC + j * SUB
            dp_scr[lax.rem(c + par1, 2), pl.ds(j * SUB, SUB), :] = jnp.dot(
                v_ref[rows_of(base1 + off, SUB), :], do_scr[a], preferred_element_type=f32
            )

    def sums(c, slot, base, par):
        qt = q_scr[slot]
        dot = do_scr[slot]
        delta = de_scr[slot]
        dq = dq_scr[...]
        for j in range(KC // SUB):
            off = c * KC + j * SUB
            p = p_scr[slot, rows_of(off, SUB), :]
            dp = dp_scr[lax.rem(c + par, 2), pl.ds(j * SUB, SUB), :]
            ds = (p.astype(f32) * (dp - delta)).astype(bf16)
            keys = rows_of(base + off, SUB)
            dv_ref[:, keys] += lax.dot_general(
                dot, p, (((1,), (1,)), ((), ())), preferred_element_type=f32
            )
            dk_ref[:, keys] += lax.dot_general(
                qt, ds, (((1,), (1,)), ((), ())), preferred_element_type=f32
            )
            dq = dq + jnp.dot(kt_ref[:, keys], ds, preferred_element_type=f32)
        dq_scr[...] = dq

    def load():
        scaled = dot_ref[...].astype(f32) * linv_ref[...]
        de_scr[a] = jnp.sum(scaled * o_ref[...], axis=0, keepdims=True)
        do_scr[a] = scaled.astype(bf16)
        q_scr[a] = qt_ref[...]

    @pl.when(i == 0)
    def _():
        dk_ref[...] = jnp.zeros_like(dk_ref)
        dv_ref[...] = jnp.zeros_like(dv_ref)
        dq_scr[...] = jnp.zeros_like(dq_scr)
        fetch(0, 0)
        load()
        dp_of(0)

    @pl.when(jnp.logical_and(i > 0, i < last))
    def _():
        load()
        dp_of(0)
        sums(n2 - 1, b, base2, par2)

    @pl.when(i == last)
    def _():
        sums(n2 - 1, b, base2, par2)

    @pl.when(i > 0)
    def _():
        dq_ref[...] = dq_scr[...] * logit_scale
        dq_scr[...] = jnp.zeros_like(dq_scr)

    @pl.when(i < last)
    def _():
        def wait(c, _):
            part = pl.ds(0, KC)
            pltpu.make_async_copy(p_hbm.at[0, part], p_scr.at[a, part], sem.at[a]).wait()
            return 0

        lax.fori_loop(0, n1, wait, 0)

        @pl.when(i + 1 < last)
        def _():
            fetch(i + 1, b)

        def step(c, _):
            dp_of(c + 1)
            sums(c, a, base1, par1)
            return 0

        lax.fori_loop(0, n1 - 1, step, 0)


def attn_bwd(qt, dot, o, linv, kt, v, p, tiles, nk):
    count, base, which, parity = tile_lists(tiles, nk)
    nq = qt.shape[1]
    steps = len(tiles)

    def now(r):
        return pl.BlockSpec((r, QT), lambda i, n, b, s, e: (0, s[i]))

    def prev(r):
        return pl.BlockSpec((r, QT), lambda i, n, b, s, e: (0, s[jnp.maximum(i - 1, 0)]))

    def whole(x):
        return pl.BlockSpec(x.shape, lambda i, n, b, s, e: (0, 0))

    sums = jax.ShapeDtypeStruct(kt.shape, f32)
    work = pair_units(tiles)
    return pl.pallas_call(
        bwd_kernel,
        name="attn_bwd",
        grid_spec=pltpu.PrefetchScalarGridSpec(
            num_scalar_prefetch=4,
            grid=(steps + 1,),
            in_specs=[
                now(HEAD_DIM),
                now(HEAD_DIM),
                now(HEAD_DIM),
                now(1),
                whole(kt),
                whole(v),
                pl.BlockSpec(memory_space=pl.ANY),
            ],
            out_specs=[prev(HEAD_DIM), whole(sums), whole(sums)],
            scratch_shapes=[
                pltpu.VMEM((2, nk, QT), bf16),
                pltpu.VMEM((2, KC, QT), f32),
                pltpu.VMEM((2, HEAD_DIM, QT), bf16),
                pltpu.VMEM((2, HEAD_DIM, QT), bf16),
                pltpu.VMEM((2, 1, QT), f32),
                pltpu.VMEM((HEAD_DIM, QT), f32),
                pltpu.SemaphoreType.DMA((2,)),
            ],
        ),
        out_shape=[jax.ShapeDtypeStruct((HEAD_DIM, nq), f32), sums, sums],
        compiler_params=pltpu.CompilerParams(vmem_limit_bytes=VMEM),
        cost_estimate=pl.CostEstimate(
            flops=work * 2048, bytes_accessed=work * 2, transcendentals=0
        ),
    )(count, base, which, parity, qt, dot, o, linv, kt, v, p)


def swap(x, axis, distance):
    return lax.ppermute(x, axis, [(i, i ^ distance) for i in range(lax.axis_size(axis))])


def gather_seq(x):
    cycle = lax.axis_size("seq")
    even = [x] + [swap(x, "seq", d) for d in range(2, cycle, 2)]
    odd = [swap(block, "seq", 1) for block in even]
    blocks = []
    for one, two in zip(even, odd):
        blocks += [one, two]
    return jnp.stack(blocks)


def in_order(stack, axis):
    me = lax.axis_index(axis)
    return jnp.take(stack, me ^ lax.iota(jnp.int32, stack.shape[0]), axis=0)


def scatter_sum_seq(x):
    cycle = lax.axis_size("seq")
    me = lax.axis_index("seq")
    halves = x.reshape(cycle // 2, 2, *x.shape[1:])
    mine = lax.dynamic_index_in_dim(halves, me % 2, 1, keepdims=False)
    other = lax.dynamic_index_in_dim(halves, 1 - me % 2, 1, keepdims=False)
    chip = (mine.astype(f32) + swap(other, "seq", 1).astype(f32)).astype(bf16)
    total = lax.dynamic_index_in_dim(chip, me // 2, 0, keepdims=False).astype(f32)
    for d in range(1, cycle // 2):
        part = lax.dynamic_index_in_dim(chip, (me // 2) ^ d, 0, keepdims=False)
        total = total + swap(part, "seq", 2 * d).astype(f32)
    return total


def sum_small(x):
    for axis in ("exp", "seq"):
        d = 1
        while d < lax.axis_size(axis):
            x = x + swap(x, axis, d)
            d *= 2
    return x


def layer_norm(values, gain, shift):
    centre = jnp.mean(values, axis=-1, keepdims=True)
    centered = values - centre
    spread = jnp.mean(centered * centered, axis=-1, keepdims=True)
    return centered * lax.rsqrt(spread + norm_eps) * gain + shift


def own_quarters(x, parity, cycle):
    cut = x.reshape(*x.shape[:-1], cycle, 4, x.shape[-1] // (4 * cycle))
    outer = jnp.concatenate([cut[..., 0:1, :], cut[..., 3:4, :]], axis=-2)
    picked = jnp.where(parity == 0, outer, cut[..., 1:3, :])
    return picked.reshape(*x.shape[:-1], x.shape[-1] // 2)


def to_owners(units, span):
    quarter = span // 4
    one, mid, two = units[:, 0], units[:, 1], units[:, 2]
    outer = jnp.concatenate([mid[..., :quarter], mid[..., 3 * quarter :]], axis=-1)
    inner = mid[..., quarter : 3 * quarter]
    even = jnp.concatenate([one, outer], axis=-1)
    odd = jnp.concatenate([two, inner], axis=-1)
    both = jnp.stack([even, odd], axis=1)
    return both.reshape(both.shape[0] * 2, *both.shape[2:])


def from_owners(got, span):
    quarter = span // 4
    both = got.reshape(got.shape[0] // 2, 2, *got.shape[1:])
    outer, inner = both[:, 0, ..., span:], both[:, 1, ..., span:]
    mid = jnp.concatenate([outer[..., :quarter], inner, outer[..., quarter:]], axis=-1)
    return jnp.stack([both[:, 0, ..., :span], mid, both[:, 1, ..., :span]], axis=1)


def local(
    inputs,
    token_ids,
    hash_table,
    capacity,
    ln1_gain,
    ln1_bias,
    w_qkv,
    q_bias,
    v_bias,
    w_out,
    out_bias,
    ln2_gain,
    ln2_bias,
    up_weight,
    up_bias,
    down_weight,
    down_bias,
    out_grad,
):
    nseq, span, width = inputs.shape
    tokens = nseq * span
    cycle = lax.axis_size("seq")
    nexp = lax.axis_size("exp")
    me = lax.axis_index("seq")
    parity = me % 2
    pair = me // 2
    pairs = cycle // 2
    nk = cycle * span
    assert nseq * HEADS == 3 * pairs

    experts = capacity.shape[0]
    cap = 5 * tokens // (4 * experts)
    expert_of = jnp.take(hash_table, token_ids.reshape(tokens))
    onehot = (expert_of[:, None] == lax.iota(jnp.int32, experts)[None, :]).astype(jnp.int32)
    rank = jnp.sum(onehot * (jnp.cumsum(onehot, axis=0) - 1), axis=1)
    kept = rank < jnp.take(capacity, expert_of)
    slot = jnp.where(kept, expert_of * cap + rank, experts * cap)
    fetch = jnp.minimum(slot, experts * cap - 1)

    def to_experts(rows):
        sent = jnp.zeros((experts * cap, width), bf16).at[slot].set(rows, mode="drop")
        return lax.all_to_all(sent, "exp", split_axis=0, concat_axis=0, tiled=True)

    def from_experts(rows):
        back = lax.all_to_all(rows, "exp", split_axis=0, concat_axis=0, tiled=True)
        return jnp.where(kept[:, None], jnp.take(back, fetch, axis=0).astype(f32), 0.0)

    grad_rows = out_grad.reshape(tokens, width)

    mine = (3 * pair) // HEADS
    stack = gather_seq(inputs)
    blocks = lax.dynamic_index_in_dim(in_order(stack, "seq"), mine, 1, keepdims=False)
    h1 = layer_norm(blocks.reshape(nk, width).astype(f32), ln1_gain, ln1_bias).astype(bf16)

    head_full = (3 * pair + 2 * parity) % HEADS
    head_half = (3 * pair + 1) % HEADS
    w_heads = w_qkv.reshape(width, 3, HEADS, HEAD_DIM)

    def of_head(x, axis):
        return jnp.stack(
            [
                lax.dynamic_index_in_dim(x, head_full, axis, keepdims=False),
                lax.dynamic_index_in_dim(x, head_half, axis, keepdims=False),
            ]
        )

    w_mine = of_head(w_heads, 2)
    qb = of_head(q_bias.reshape(HEADS, HEAD_DIM), 0)
    vb = of_head(v_bias.reshape(HEADS, HEAD_DIM), 0)
    bias = jnp.stack([qb, jnp.zeros_like(qb), vb], axis=1)
    w_rows = w_mine.transpose(0, 2, 3, 1).reshape(6 * HEAD_DIM, width)
    flat = lax.dot_general(w_rows, h1, (((1,), (1,)), ((), ())), preferred_element_type=f32)
    proj = (flat + bias.reshape(6 * HEAD_DIM, 1)).astype(bf16).reshape(2, 3, HEAD_DIM, nk)
    qt = jnp.concatenate([proj[0, 0], own_quarters(proj[1, 0], parity, cycle)], axis=1)
    kt = jnp.concatenate([proj[0, 1], proj[1, 1]], axis=1)
    vt = jnp.concatenate([proj[0, 2], proj[1, 2]], axis=1)
    k, v = kt.T, vt.T
    order = lax.broadcasted_iota(jnp.int32, (1, nk), 1)
    place = jnp.concatenate([order, own_quarters(order, parity, cycle)], axis=1)
    full = [(i, 0, (i * QT + QT + KC - 1) // KC) for i in range(nk // QT)]
    half = [(nk // QT + i, 1, (2 * (i * QT + QT) + KC - 1) // KC) for i in range(nk // (2 * QT))]
    tiles = sorted(full + half, key=lambda t: t[2])
    attn, linv, p = attn_fwd(qt, k, vt, place, tiles, nk)

    def send_home(full_part, half_part):
        rows = full_part.shape[0]
        joined = jnp.concatenate(
            [full_part.reshape(rows, cycle, span), half_part.reshape(rows, cycle, span // 2)],
            axis=2,
        )
        got = lax.all_to_all(
            joined.transpose(1, 0, 2), "seq", split_axis=0, concat_axis=0, tiled=True
        )
        return from_owners(got, span)

    low = attn.astype(bf16)
    attn_low = send_home(low[:, :nk], low[:, nk:]).reshape(nseq, width, span)
    x_rows = inputs.reshape(tokens, width).astype(f32)
    middle = (
        x_rows
        + jnp.einsum("nht,hd->ntd", attn_low, w_out, preferred_element_type=f32).reshape(
            tokens, width
        )
        + out_bias
    )
    normed2, norm2_back = jax.vjp(layer_norm, middle, ln2_gain, ln2_bias)

    dy = to_experts(grad_rows)
    rows = to_experts(normed2.astype(bf16))
    up, down = up_weight[0], down_weight[0]
    z = jnp.dot(rows, up, preferred_element_type=f32) + up_bias[0]
    phi = 0.5 * (1.0 + lax.erf(z * (1.0 / math.sqrt(2.0))))
    hidden = (z * phi).astype(bf16)
    slope = phi + z * jnp.exp(-0.5 * z * z) * (1.0 / math.sqrt(2.0 * math.pi))
    da = lax.dot_general(dy, down, (((1,), (1,)), ((), ())), preferred_element_type=f32)
    dz = (da * slope).astype(bf16)
    dh2 = lax.dot_general(dz, up, (((1,), (1,)), ((), ())), preferred_element_type=f32)
    grad_normed2 = from_experts(dh2.astype(bf16))
    y = jnp.dot(hidden, down, preferred_element_type=f32) + down_bias[0]
    output = (middle + from_experts(y.astype(bf16))).astype(bf16).reshape(nseq, span, width)
    contract0 = (((0,), (0,)), ((), ()))
    grad_up = lax.dot_general(rows, dz, contract0, preferred_element_type=f32).astype(bf16)
    grad_down = lax.dot_general(hidden, dy, contract0, preferred_element_type=f32).astype(bf16)
    grad_up_bias = jnp.sum(dz, axis=0, dtype=f32)
    grad_down_bias = jnp.sum(dy, axis=0, dtype=f32)
    ff = up.shape[1]
    up_sum = scatter_sum_seq(grad_up.reshape(width, cycle, ff // cycle).transpose(1, 0, 2))
    down_sum = scatter_sum_seq(grad_down.reshape(cycle, ff // cycle, width))
    bias_sum = scatter_sum_seq(
        jnp.concatenate(
            [grad_up_bias.reshape(cycle, ff // cycle), grad_down_bias.reshape(cycle, width // cycle)],
            axis=1,
        )
    )

    grad_mid_norm, grad_ln2_gain, grad_ln2_bias = norm2_back(grad_normed2)
    grad_middle = grad_rows.astype(f32) + grad_mid_norm
    grad_branch = grad_middle.astype(bf16)
    branch = grad_branch.reshape(nseq, span, width)
    do_home = jnp.einsum("hd,ntd->nht", w_out, branch, preferred_element_type=f32).astype(bf16)
    sent = to_owners(do_home.reshape(pairs, 3, HEAD_DIM, span), span)
    got = lax.all_to_all(sent, "seq", split_axis=0, concat_axis=0, tiled=True)
    got = got.transpose(1, 0, 2)
    dot = jnp.concatenate(
        [got[..., :span].reshape(HEAD_DIM, nk), got[..., span:].reshape(HEAD_DIM, nk // 2)], axis=1
    )
    dq, dk, dv = attn_bwd(qt, dot, attn, linv, kt, v, p, tiles, nk)
    dk = dk * logit_scale
    both = jnp.stack([dk[:, nk:], dv[:, nk:]])
    other = swap(own_quarters(both, 1 - parity, cycle).astype(bf16), "seq", 1)
    both = own_quarters(both, parity, cycle) + other.astype(f32)
    part_full = jnp.concatenate([dq[:, :nk], dk[:, :nk], dv[:, :nk]], axis=0).astype(bf16)
    part_half = jnp.concatenate([dq[:, nk:], both[0], both[1]], axis=0).astype(bf16)
    units = send_home(part_full, part_half).reshape(nseq, HEADS, 3, HEAD_DIM, span)
    grad_normed = jnp.einsum(
        "nhcet,dche->ntd", units, w_heads, preferred_element_type=f32
    ).reshape(tokens, width)
    bias_grads = jnp.sum(units, axis=(0, 4), dtype=f32)
    grad_q_bias = bias_grads[:, 0].reshape(width)
    grad_v_bias = bias_grads[:, 2].reshape(width)
    _, norm1_back = jax.vjp(layer_norm, x_rows, ln1_gain, ln1_bias)
    grad_from_norm, grad_ln1_gain, grad_ln1_bias = norm1_back(grad_normed)
    input_grad = (grad_middle + grad_from_norm).reshape(nseq, span, width)

    h1_half = own_quarters(h1.T, parity, cycle).T
    grad_full = jnp.dot(part_full, h1, preferred_element_type=f32).astype(bf16)
    grad_half = jnp.dot(part_half, h1_half, preferred_element_type=f32).astype(bf16)
    cut = 3 * HEAD_DIM // 2
    grad_half = grad_half.reshape(2, cut, width)
    own = lax.dynamic_index_in_dim(grad_half, parity, 0, keepdims=False)
    away = lax.dynamic_index_in_dim(grad_half, 1 - parity, 0, keepdims=False)
    own = (own.astype(f32) + swap(away, "seq", 1).astype(f32)).astype(bf16)
    grad_w = jnp.concatenate([grad_full, own], axis=0)
    grad_w_out = lax.dot_general(
        attn_low.transpose(0, 2, 1).reshape(tokens, width),
        grad_branch,
        contract0,
        preferred_element_type=f32,
    )
    grad_w_out = scatter_sum_seq(
        grad_w_out.astype(bf16).reshape(cycle, width // cycle, width)
    ).astype(bf16)
    piece = jnp.concatenate([grad_w, grad_w_out], axis=0)
    count = piece.shape[0]
    spread = lax.all_to_all(piece, "exp", split_axis=0, concat_axis=0, tiled=True)
    summed = jnp.sum(spread.reshape(nexp, count // nexp, width), axis=0, dtype=f32).astype(bf16)
    column = jnp.stack([summed] + [swap(summed, "exp", d) for d in range(1, nexp)])
    column = in_order(column, "exp").reshape(count, width)
    everyone = in_order(gather_seq(column), "seq")
    g_full = everyone[:, : 3 * HEAD_DIM].reshape(pairs, 2, 3 * HEAD_DIM, width)
    g_half = everyone[:, 3 * HEAD_DIM : 3 * HEAD_DIM + cut].reshape(pairs, 3 * HEAD_DIM, width)
    g_units = jnp.stack([g_full[:, 0], g_half, g_full[:, 1]], axis=1)
    g_units = g_units.reshape(nseq, HEADS, 3, HEAD_DIM, width).astype(f32).sum(axis=0)
    grad_w_qkv = g_units.transpose(3, 1, 0, 2).reshape(width, 3 * width)
    grad_w_out = everyone[:, 3 * HEAD_DIM + cut :].reshape(width, width).astype(f32)

    small = sum_small(
        jnp.stack(
            [
                grad_ln1_gain,
                grad_ln1_bias,
                grad_q_bias,
                grad_v_bias,
                jnp.sum(grad_branch, axis=0, dtype=f32),
                grad_ln2_gain,
                grad_ln2_bias,
            ]
        )
    )
    share = ff // cycle
    return (
        output,
        input_grad,
        small[0],
        small[1],
        grad_w_qkv,
        small[2],
        small[3],
        grad_w_out,
        small[4],
        small[5],
        small[6],
        up_sum[None],
        bias_sum[None, :share],
        down_sum[None],
        bias_sum[None, share:],
    )


def solution(mesh):
    in_specs = (
        P("exp", "seq", None),
        P("exp", "seq"),
        P(),
        P(),
        P(),
        P(),
        P(),
        P(),
        P(),
        P(),
        P(),
        P(),
        P(),
        P("exp", None, None),
        P("exp", None),
        P("exp", None, None),
        P("exp", None),
        P("exp", "seq", None),
    )
    out_specs = (
        P("exp", "seq", None),
        P("exp", "seq", None),
        P(),
        P(),
        P(),
        P(),
        P(),
        P(),
        P(),
        P(),
        P(),
        P("exp", None, "seq"),
        P("exp", "seq"),
        P("exp", "seq", None),
        P("exp", "seq"),
    )
    return jax.shard_map(local, mesh=mesh, in_specs=in_specs, out_specs=out_specs, check_vma=False)
```

time: 1080 us -> 574 us (0.53)
  matrix products: 450 us -> 58.1 us
  waiting for transfers between devices: 283 us -> 116 us
  Pallas kernels: 0 us -> 84.6 us
  blocking collectives: 42.6 us -> 0 us
  local copies, waits for them, and re-layouts: 107 us -> 142 us
  other arithmetic: 134 us -> 99.7 us
  starting transfers between devices: 37.9 us -> 64.8 us
  between operations: 15.1 us -> 2.4 us
    dot_general x47 -> x13, matrix products: 450 us -> 58.1 us  [the longest x1 8.48 us: local(): lax.dot_general(hidden, dy, contract0, preferred_element_type=f32)]
    psum x1 -> x0, waiting for transfers between devices: 142 us -> none  [local(): lax.psum((grad_ln1_gain, grad_ln1_bias, grad_w_qkv, grad_q_bias, grad_v_b...]
    pallas_call x0 -> x2, Pallas kernels: none -> 84.6 us  [the longest x1 51.3 us: attn_bwd(): pl.pallas_call(bwd_kernel, name='attn_bwd', grid_spec=pltpu.PrefetchScala...]
    psum x1 -> x0, blocking collectives: 42.6 us -> none  [local(): lax.psum((grad_ln1_gain, grad_ln1_bias, grad_w_qkv, grad_q_bias, grad_v_b...]
    reduce_sum x13 -> x4, other arithmetic: 41.6 us -> 2.3 us  [the longest x1 1.4 us: local(): grad_down_bias = jnp.sum(dy, axis=0, dtype=f32)]
    reduce_scatter x2 -> x0, waiting for transfers between devices: 38.5 us -> none  [the longest x1 38.5 us: local(): lax.psum_scatter(grad_down.astype(jnp.bfloat16), 'seq', scatter_dimension...]
    all_to_all x4 -> x8, starting transfers between devices: 18.3 us -> 35.5 us  [the longest x2 11.1 us: to_experts(): return lax.all_to_all(sent, 'exp', split_axis=0, concat_axis=0, tiled=True)]
    while x35 -> x0, local copies, waits for them, and re-layouts: 14.5 us -> none
  transfers between devices with their start and end apart: 43 -> 48, of which waited for: 12 -> 20; matrix products, arithmetic and copies ran while one was open for 56% -> 43% of each run, Pallas kernels for 0% -> 15%
where the time goes in v1:
time: 574 us; the launch traced here: 567 us
  local copies, waits for them, and re-layouts  142 us (25%)
  waiting for transfers between devices  116 us (20%)
  other arithmetic  99.7 us (17%)
  Pallas kernels  84.6 us (15%)
  starting transfers between devices  64.8 us (11%)
  matrix products  58.1 us (10%)
    ppermute x40, waiting for transfers between devices, swap(): lax.ppermute(x, axis, [(i, i ^ distance) for i in range(lax.axis_size(axi...  77.4 us
    pallas_call x1, Pallas kernels, attn_bwd(): pl.pallas_call(bwd_kernel, name='attn_bwd', grid_spec=pltpu.PrefetchScala...  51.3 us
    unnamed x164, local copies, waits for them, and re-layouts  49.5 us
    pallas_call x1, Pallas kernels, attn_fwd(): pl.pallas_call(fwd_kernel, name='attn_fwd', grid_spec=pltpu.PrefetchScala...  33.3 us
    ppermute x40, starting transfers between devices, swap(): lax.ppermute(x, axis, [(i, i ^ distance) for i in range(lax.axis_size(axi...  29.4 us
    convert_element_type x2, other arithmetic, local(): layer_norm(blocks.reshape(nk, width).astype(f32), ln1_gain, ln1_bias)  16.2 us
    gather x3, local copies, waits for them, and re-layouts, in_order(): return jnp.take(stack, me ^ lax.iota(jnp.int32, stack.shape[0]), axis=0)  12.6 us
    all_to_all x2, waiting for transfers between devices, from_experts(): back = lax.all_to_all(rows, 'exp', split_axis=0, concat_axis=0, tiled=True)  11.5 us
  transfers between devices with their start and end apart: 48, of which 20 were waited for; matrix products, arithmetic and copies ran while one was open for 43% of the time, Pallas kernels for 15%

profile of v1, /device:TPU:0, one launch (start us, length us, event | category | flops | bytes accessed | tf_op | source)
XLA Modules:
  0.0 567.5 jit_solution(16833104126758661334)
XLA Ops:
  6.0 3.6 gather_fusion.1
  14.1 3.3 compare_select_fusion
  17.4 3.7 scatter_custom_fusion.1
  21.1 5.8 %all-to-all-start.3 = ((bf16[4,160,768]{2,1,0:T(8,128)(2,1)}), bf16[4,160,768]{2,1,0:T(8,128)(2,1)}, u32[]{:S(2)}, u32[]{:S(2)}) async-start(bf16[4,160,768]{2,1,0:T(8,128)(2,1)} %bitcast.58), calls=%async_computation.3 | async-start | bytes 1966080 | tf_op jit(solution)/shard_map/all_to_all | solution.py:499
  27.1 5.8 %copy.99 = bf16[768,2304]{0,1:T(8,128)(2,1)} copy(bf16[768,2304]{1,0:T(8,128)(2,1)} %param.33) | data formatting | bytes 7077888 | tf_op args[6]
  51.0 6.4 %gather_fusion = bf16[8,512,768]{2,1,0:T(8,128)(2,1)} fusion(bf16[8,512,768]{2,1,0:T(8,128)(2,1)} %bitcast.14, s32[1024]{0:T(1024)S(1)} %pad_clamp_fusion.3), kind=kCustom, calls=%fused_computation.2 | custom fusion | bytes 12582944 | tf_op jit(solution)/shard_map/jit(_take)/gather | solution.py:398
  57.3 4.3 convert_reduce_fusion
  65.3 10.1 %fusion.5 = bf16[8,1,512,768]{3,2,0,1:T(8,128)(2,1)S(1)} fusion(f32[768]{0:T(1024)S(1)} %copy-done.39, f32[768]{0:T(1024)S(1)} %copy-done.31, f32[8,512]{1,0:T(8,128)S(1)} %get-tuple-element.160, f32[8,512]{1,0:T(8,128)S(1)} %get-tuple-element.158, bf16[8,512,768]{2,1,0:T(8,128)(2,1)S(1)} %copy-done.2, pred[8]{0:T(512)(128)(4,1)S(1)} %compare_and_fusion.2), kind=kLoop, calls=%fused_computation.15 | loop fusion | flops 22020096 | bytes 12621832 | tf_op jit(solution)/shard_map/convert_element_type | solution.py:510
  90.4 3.8 fusion.97
  97.8 33.3 %attn_fwd.1 = (f32[64,6144]{1,0:T(8,128)}, f32[1,6144]{1,0:T(1,128)}, bf16[12,4096,512]{2,1,0:T(8,128)(2,1)}) custom-call(s32[13]{0:T(128)} %constant.325.clone.n_ref, s32[13]{0:T(128)} %constant.326.clone.base_ref, s32[13]{0:T(128)} %constant.327.clone.tile_ref, bf16[64,6144]{1,0:T(8,128)(2,1)} %pad_maximum_fusion.5.q_ref.qt_ref, ...), custom_call_target="tpu_custom_call" | custom-call | flops 16106127360 | bytes 31457280 | tf_op jit(solution)/shard_map/attn_fwd/pallas_call | solution.py:182
  133.7 3.5 all-to-all-start
  143.9 5.9 %all-to-all-done = bf16[8,64,768]{2,1,0:T(8,128)(2,1)S(1)} async-done(((bf16[8,64,768]{2,1,0:T(8,128)(2,1)}), bf16[8,64,768]{2,1,0:T(8,128)(2,1)S(1)}, u32[]{:S(2)}, u32[]{:S(2)}) %all-to-all-start) | async-done | bytes 786464 | tf_op jit(solution)/shard_map/all_to_all | solution.py:548
  151.4 4.1 scatter_custom_fusion
  155.5 5.3 all-to-all-start.1
  160.9 6.1 %add_convert_fusion = bf16[4096,768]{1,0:T(8,128)(2,1)S(1)} fusion(bf16[8,512,768]{2,1,0:T(8,128)(2,1)} %gather_fusion, f32[768]{0:T(1024)S(1)} %copy-done.40, f32[768]{0:T(1024)S(1)} %copy-done.31, f32[4096]{0:T(1024)S(1)} %bitcast.473, f32[4096]{0:T(1024)S(1)} %bitcast.474, pred[4096]{0:T(1024)(128)(4,1)S(1)} %bitcast.480), kind=kLoop, calls=%fused_computation.16 | loop fusion | flops 22020096 | bytes 12625920 | tf_op jit(solution)/shard_map/convert_element_type | solution.py:510
  171.5 10.8 %all-to-all-done.1 = bf16[4,160,768]{2,1,0:T(8,128)(2,1)} async-done(((bf16[4,160,768]{2,1,0:T(8,128)(2,1)}), bf16[4,160,768]{2,1,0:T(8,128)(2,1)}, u32[]{:S(2)}, u32[]{:S(2)}) %all-to-all-start.1) | async-done | bytes 983072 | tf_op jit(solution)/shard_map/all_to_all | solution.py:499
  182.4 7.2 %multiply_convert_fusion = (bf16[640,3072]{1,0:T(8,128)(2,1)}, f32[640,3072]{1,0:T(8,128)S(1)}) fusion(f32[3072]{0:T(1024)S(1)} %bitcast.493, bf16[640,768]{1,0:T(8,128)(2,1)} %bitcast.50, bf16[1,768,3072]{2,1,0:T(8,128)(2,1)} %param.40), kind=kOutput, calls=%fused_computation.25 | convolution fusion | flops 3031695360 | bytes 17510400 | tf_op jit(solution)/shard_map/dot_general | solution.py:568
  189.6 7.9 %convert_reduce_fusion.1 = (f32[3072]{0:T(1024)S(1)}, bf16[640,3072]{1,0:T(8,128)(2,1)S(1)}) fusion(f32[640,3072]{1,0:T(8,128)S(1)} %get-tuple-element.177, f32[3072]{0:T(1024)S(1)} %bitcast.494, bf16[640,768]{1,0:T(8,128)(2,1)} %bitcast.59, bf16[1,3072,768]{2,1,0:T(8,128)(2,1)S(1)} %bitcast.492), kind=kOutput, calls=%fused_computation.24 | convolution fusion | flops 3045454848 | bytes 17522688 | tf_op jit(solution)/shard_map/dot_general | solution.py:572
  197.6 4.2 fusion.44
  201.8 3.5 all-to-all-start.4
  205.3 6.3 %convolution_convert_fusion.1 = bf16[768,3072]{1,0:T(8,128)(2,1)S(1)} fusion(bf16[640,768]{1,0:T(8,128)(2,1)} %bitcast.50, bf16[640,3072]{1,0:T(8,128)(2,1)} %copy-done.62), kind=kOutput, calls=%fused_computation.32 | convolution fusion | flops 3022258176 | bytes 9633792 | tf_op jit(solution)/shard_map/dot_general | solution.py:579
  215.3 6.6 %add_convert_fusion.2 = bf16[640,768]{1,0:T(8,128)(2,1)} fusion(bf16[640,3072]{1,0:T(8,128)(2,1)S(1)} %copy-done.63, bf16[1,3072,768]{2,1,0:T(8,128)(2,1)} %param.42, f32[768]{0:T(1024)S(1)} %copy-done.55), kind=kOutput, calls=%fused_computation.59 | convolution fusion | flops 3020881920 | bytes 9636864 | tf_op jit(solution)/shard_map/dot_general | solution.py:576
  221.9 6.5 %all-to-all-done.4 = bf16[4,160,768]{2,1,0:T(8,128)(2,1)S(1)} async-done(((bf16[4,160,768]{2,1,0:T(8,128)(2,1)}), bf16[4,160,768]{2,1,0:T(8,128)(2,1)S(1)}, u32[]{:S(2)}, u32[]{:S(2)}) %all-to-all-start.4) | async-done | bytes 983072 | tf_op jit(solution)/shard_map/all_to_all | solution.py:502
  228.4 3.7 all-to-all-start.2
  232.1 3.3 dynamic-slice_bitcast_fusion.1
  236.1 8.5 %convolution_convert_fusion = bf16[3072,768]{1,0:T(8,128)(2,1)} fusion(bf16[640,3072]{1,0:T(8,128)(2,1)} %get-tuple-element.176, bf16[640,768]{1,0:T(8,128)(2,1)} %bitcast.59), kind=kOutput, calls=%fused_computation.31 | convolution fusion | flops 3022258176 | bytes 9633792 | tf_op jit(solution)/shard_map/dot_general | solution.py:580
  250.8 5.0 all-to-all-done.2
  258.6 3.4 fusion.99
  270.9 5.6 all-to-all-start.5
  276.6 3.3 dynamic-slice_bitcast_fusion
  286.0 3.7 all-to-all-done.5
  290.7 51.3 %attn_bwd.1 = (f32[64,6144]{1,0:T(8,128)}, f32[64,8192]{1,0:T(8,128)}, f32[64,8192]{1,0:T(8,128)}) custom-call(s32[13]{0:T(128)} %constant.325.clone.n_ref, s32[13]{0:T(128)} %constant.326.clone.base_ref, s32[13]{0:T(128)} %constant.327.clone.tile_ref, s32[13]{0:T(128)} %constant.328.clone.parity_ref, bf16[64,6144]{1,0:T(8,128)(2,1)} %pad_maximum_fusion.5.q_ref.qt_ref, ...), custom_call_target="tpu_custom_call" | custom-call | flops 32212254720 | bytes 31457280 | tf_op jit(solution)/shard_map/attn_bwd/pallas_call | solution.py:348
  356.9 3.3 fusion.105
  360.2 3.7 select_convert_fusion
  367.4 5.5 fusion.48
  387.6 3.5 all-to-all-start.7
  394.5 4.4 fusion.13
  400.7 6.5 %all-to-all-done.7 = bf16[4,96,768]{2,1,0:T(8,128)(2,1)S(1)} async-done(((bf16[4,96,768]{2,1,0:T(8,128)(2,1)}), bf16[4,96,768]{2,1,0:T(8,128)(2,1)S(1)}, u32[]{:S(2)}, u32[]{:S(2)}) %all-to-all-start.7) | async-done | bytes 589856 | tf_op jit(solution)/shard_map/all_to_all | solution.py:642
  407.2 4.5 all-to-all-start.6
  423.4 30.5 %collective-permute-done.35 = bf16[480]{0:T(512)(128)(2,1)S(1)} collective-permute-done((bf16[480]{0:T(512)(128)(2,1)S(1)}, bf16[480]{0:T(512)(128)(2,1)S(1)}, u32[]{:S(2)}, u32[]{:S(2)}) %collective-permute-start.35) | collective-permute-done | bytes 992 | tf_op jit(solution)/shard_map/ppermute | solution.py:383
  461.5 4.5 collective-permute-done.30
  465.9 4.2 collective-permute-done.29
  474.1 8.8 %collective-permute-done.39 = bf16[384,768]{1,0:T(8,128)(2,1)} collective-permute-done((bf16[384,768]{1,0:T(8,128)(2,1)}, bf16[384,768]{1,0:T(8,128)(2,1)}, u32[]{:S(2)}, u32[]{:S(2)}) %collective-permute-start.39) | collective-permute-done | bytes 589856 | tf_op jit(solution)/shard_map/ppermute | solution.py:383
  482.9 7.9 %collective-permute-done.38 = bf16[384,768]{1,0:T(8,128)(2,1)} collective-permute-done((bf16[384,768]{1,0:T(8,128)(2,1)}, bf16[384,768]{1,0:T(8,128)(2,1)}, u32[]{:S(2)}, u32[]{:S(2)}) %collective-permute-start.38) | collective-permute-done | bytes 589856 | tf_op jit(solution)/shard_map/ppermute | solution.py:383
  490.8 3.3 collective-permute-done.37
  523.7 5.1 collective-permute-done.24
  544.1 5.5 gather_fusion.3
  557.6 8.1 %copy.126 = f32[768,2304]{1,0:T(8,128)} copy(f32[768,2304]{0,1:T(8,128)} %bitcast.414) | data formatting | bytes 14155776
  (415 shorter events, 210.0 us)
Async XLA Ops:
  0.7 40.4 %collective-permute-start = (bf16[1,512,768]{2,1,0:T(8,128)(2,1)}, bf16[1,512,768]{2,1,0:T(8,128)(2,1)}, u32[]{:S(2)}, u32[]{:S(2)}) collective-permute-start(bf16[1,512,768]{2,1,0:T(8,128)(2,1)} %param.27), channel_id=1, source_target_pairs={{0,4},{4,0},{8,12},{12,8},{16,20},{20,16},{24,28},{28,24},{1,5},{5... | collective-permute-start | bytes 2359304 | tf_op jit(solution)/shard_map/ppermute | solution.py:383
  1.2 35.1 %collective-permute-start.1 = (bf16[1,512,768]{2,1,0:T(8,128)(2,1)}, bf16[1,512,768]{2,1,0:T(8,128)(2,1)}, u32[]{:S(2)}, u32[]{:S(2)}) collective-permute-start(bf16[1,512,768]{2,1,0:T(8,128)(2,1)} %param.27), channel_id=1, source_target_pairs={{0,8},{4,12},{8,0},{12,4},{16,24},{20,28},{24,16},{28,20},{1,9},{5... | collective-permute-start | bytes 2359304 | tf_op jit(solution)/shard_map/ppermute | solution.py:383
  3.8 36.8 %collective-permute-start.3 = (bf16[1,512,768]{2,1,0:T(8,128)(2,1)}, bf16[1,512,768]{2,1,0:T(8,128)(2,1)}, u32[]{:S(2)}, u32[]{:S(2)}) collective-permute-start(bf16[1,512,768]{2,1,0:T(8,128)(2,1)} %param.27), channel_id=1, source_target_pairs={{0,16},{4,20},{8,24},{12,28},{16,0},{20,4},{24,8},{28,12},{1,17},{... | collective-permute-start | bytes 2359304 | tf_op jit(solution)/shard_map/ppermute | solution.py:383
  5.3 35.3 %collective-permute-start.5 = (bf16[1,512,768]{2,1,0:T(8,128)(2,1)}, bf16[1,512,768]{2,1,0:T(8,128)(2,1)S(1)}, u32[]{:S(2)}, u32[]{:S(2)}) collective-permute-start(bf16[1,512,768]{2,1,0:T(8,128)(2,1)} %param.27), channel_id=1, source_target_pairs={{0,24},{4,28},{8,16},{12,20},{16,8},{20,12},{24,0},{28,4},{1,25},{... | collective-permute-start | bytes 2359304 | tf_op jit(solution)/shard_map/ppermute | solution.py:383
  21.1 112.6 %all-to-all-start.3 = ((bf16[4,160,768]{2,1,0:T(8,128)(2,1)}), bf16[4,160,768]{2,1,0:T(8,128)(2,1)}, u32[]{:S(2)}, u32[]{:S(2)}) async-start(bf16[4,160,768]{2,1,0:T(8,128)(2,1)} %bitcast.58), calls=%async_computation.3 | async-start | bytes 1966080 | tf_op jit(solution)/shard_map/all_to_all | solution.py:499
  36.3 8.9 %collective-permute-start.2 = (bf16[1,512,768]{2,1,0:T(8,128)(2,1)}, bf16[1,512,768]{2,1,0:T(8,128)(2,1)S(1)}, u32[]{:S(2)}, u32[]{:S(2)}) collective-permute-start(bf16[1,512,768]{2,1,0:T(8,128)(2,1)} %collective-permute-done.1), channel_id=1, source_target_pairs={{0,4},{4,0},{8,12},{12,8},{16,20},{20,16},{24,28},{28,24},{1,5},{5... | collective-permute-start | bytes 2359304 | tf_op jit(solution)/shard_map/ppermute | solution.py:383
  40.5 7.6 %collective-permute-start.4 = (bf16[1,512,768]{2,1,0:T(8,128)(2,1)}, bf16[1,512,768]{2,1,0:T(8,128)(2,1)S(1)}, u32[]{:S(2)}, u32[]{:S(2)}) collective-permute-start(bf16[1,512,768]{2,1,0:T(8,128)(2,1)} %collective-permute-done.3), channel_id=1, source_target_pairs={{0,4},{4,0},{8,12},{12,8},{16,20},{20,16},{24,28},{28,24},{1,5},{5... | collective-permute-start | bytes 2359304 | tf_op jit(solution)/shard_map/ppermute | solution.py:383
  40.5 9.5 %collective-permute-start.6 = (bf16[1,512,768]{2,1,0:T(8,128)(2,1)S(1)}, bf16[1,512,768]{2,1,0:T(8,128)(2,1)S(1)}, u32[]{:S(2)}, u32[]{:S(2)}) collective-permute-start(bf16[1,512,768]{2,1,0:T(8,128)(2,1)S(1)} %collective-permute-done.5), channel_id=1, source_target_pairs={{0,4},{4,0},{8,12},{12,8},{16,20},{20,16},{24,28},{28,24},{1,5},{5... | collective-permute-start | bytes 2359304 | tf_op jit(solution)/shard_map/ppermute | solution.py:383
  133.7 16.1 %all-to-all-start = ((bf16[8,64,768]{2,1,0:T(8,128)(2,1)}), bf16[8,64,768]{2,1,0:T(8,128)(2,1)S(1)}, u32[]{:S(2)}, u32[]{:S(2)}) async-start(bf16[8,64,768]{2,1,0:T(8,128)(2,1)} %maximum_bitcast_fusion.1), calls=%async_computation | async-start | bytes 1572864 | tf_op jit(solution)/shard_map/all_to_all | solution.py:548
  155.5 26.8 %all-to-all-start.1 = ((bf16[4,160,768]{2,1,0:T(8,128)(2,1)}), bf16[4,160,768]{2,1,0:T(8,128)(2,1)}, u32[]{:S(2)}, u32[]{:S(2)}) async-start(bf16[4,160,768]{2,1,0:T(8,128)(2,1)} %bitcast.431), calls=%async_computation.1 | async-start | bytes 1966080 | tf_op jit(solution)/shard_map/all_to_all | solution.py:499
  201.8 26.6 %all-to-all-start.4 = ((bf16[4,160,768]{2,1,0:T(8,128)(2,1)}), bf16[4,160,768]{2,1,0:T(8,128)(2,1)S(1)}, u32[]{:S(2)}, u32[]{:S(2)}) async-start(bf16[4,160,768]{2,1,0:T(8,128)(2,1)} %bitcast.60), calls=%async_computation.4 | async-start | bytes 1966080 | tf_op jit(solution)/shard_map/all_to_all | solution.py:502
  228.4 27.5 %all-to-all-start.2 = ((bf16[4,160,768]{2,1,0:T(8,128)(2,1)}), bf16[4,160,768]{2,1,0:T(8,128)(2,1)S(1)}, u32[]{:S(2)}, u32[]{:S(2)}) async-start(bf16[4,160,768]{2,1,0:T(8,128)(2,1)} %bitcast.463), calls=%async_computation.2 | async-start | bytes 1966080 | tf_op jit(solution)/shard_map/all_to_all | solution.py:502
  235.4 159.1 %collective-permute-start.28 = (bf16[4,768,384]{2,1,0:T(8,128)(2,1)}, bf16[4,768,384]{2,1,0:T(8,128)(2,1)}, u32[]{:S(2)}, u32[]{:S(2)}) collective-permute-start(bf16[4,768,384]{2,1,0:T(8,128)(2,1)} %dynamic-slice_bitcast_fusion.1), channel_id=1, source_target_pairs={{0,4},{4,0},{8,12},{12,8},{16,20},{20,16},{24,28},{28,24},{1,5},{5... | collective-permute-start | bytes 7077896 | tf_op jit(solution)/shard_map/ppermute | solution.py:383
  269.5 10.9 %collective-permute-start.14 = (bf16[4,96,768]{2,1,0:T(8,128)(2,1)}, bf16[4,96,768]{2,1,0:T(8,128)(2,1)}, u32[]{:S(2)}, u32[]{:S(2)}) collective-permute-start(bf16[4,96,768]{2,1,0:T(8,128)(2,1)} %dynamic-slice_bitcast_fusion.8), channel_id=1, source_target_pairs={{0,4},{4,0},{8,12},{12,8},{16,20},{20,16},{24,28},{28,24},{1,5},{5... | collective-permute-start | bytes 1769480 | tf_op jit(solution)/shard_map/ppermute | solution.py:383
  270.9 18.8 %all-to-all-start.5 = ((bf16[8,64,768]{2,1,0:T(8,128)(2,1)}), bf16[8,64,768]{2,1,0:T(8,128)(2,1)S(1)}, u32[]{:S(2)}, u32[]{:S(2)}) async-start(bf16[8,64,768]{2,1,0:T(8,128)(2,1)} %bitcast.437), calls=%async_computation.5 | async-start | bytes 1572864 | tf_op jit(solution)/shard_map/all_to_all | solution.py:599
  279.9 139.9 %collective-permute-start.36 = (bf16[4,384,768]{2,1,0:T(8,128)(2,1)}, bf16[4,384,768]{2,1,0:T(8,128)(2,1)}, u32[]{:S(2)}, u32[]{:S(2)}) collective-permute-start(bf16[4,384,768]{2,1,0:T(8,128)(2,1)} %dynamic-slice_bitcast_fusion), channel_id=1, source_target_pairs={{0,4},{4,0},{8,12},{12,8},{16,20},{20,16},{24,28},{28,24},{1,5},{5... | collective-permute-start | bytes 7077896 | tf_op jit(solution)/shard_map/ppermute | solution.py:383
  282.5 100.6 %collective-permute-start.17 = (bf16[96,768]{1,0:T(8,128)(2,1)}, bf16[96,768]{1,0:T(8,128)(2,1)}, u32[]{:S(2)}, u32[]{:S(2)}) collective-permute-start(bf16[96,768]{1,0:T(8,128)(2,1)} %get-tuple-element.143), channel_id=1, source_target_pairs={{0,24},{4,28},{8,16},{12,20},{16,8},{20,12},{24,0},{28,4},{1,25},{... | collective-permute-start | bytes 442376 | tf_op jit(solution)/shard_map/ppermute | solution.py:383
  285.1 98.5 %collective-permute-start.16 = (bf16[96,768]{1,0:T(8,128)(2,1)}, bf16[96,768]{1,0:T(8,128)(2,1)}, u32[]{:S(2)}, u32[]{:S(2)}) collective-permute-start(bf16[96,768]{1,0:T(8,128)(2,1)} %get-tuple-element.144), channel_id=1, source_target_pairs={{0,16},{4,20},{8,24},{12,28},{16,0},{20,4},{24,8},{28,12},{1,17},{... | collective-permute-start | bytes 442376 | tf_op jit(solution)/shard_map/ppermute | solution.py:383
  366.1 13.0 %collective-permute-start.7 = (bf16[2,64,2048]{2,1,0:T(8,128)(2,1)}, bf16[2,64,2048]{2,1,0:T(8,128)(2,1)}, u32[]{:S(2)}, u32[]{:S(2)}) collective-permute-start(bf16[2,64,2048]{2,1,0:T(8,128)(2,1)} %convert_element_type.297), channel_id=1, source_target_pairs={{0,4},{4,0},{8,12},{12,8},{16,20},{20,16},{24,28},{28,24},{1,5},{5... | collective-permute-start | bytes 1572872 | tf_op jit(solution)/shard_map/ppermute | solution.py:383
  379.1 6.5 %collective-permute-start.15 = (bf16[96,768]{1,0:T(8,128)(2,1)}, bf16[96,768]{1,0:T(8,128)(2,1)S(1)}, u32[]{:S(2)}, u32[]{:S(2)}) collective-permute-start(bf16[96,768]{1,0:T(8,128)(2,1)} %get-tuple-element.142), channel_id=1, source_target_pairs={{0,8},{4,12},{8,0},{12,4},{16,24},{20,28},{24,16},{28,20},{1,9},{5... | collective-permute-start | bytes 442376 | tf_op jit(solution)/shard_map/ppermute | solution.py:383
  383.1 8.0 %collective-permute-start.32 = (f32[4,480]{1,0:T(4,128)S(1)}, f32[4,480]{1,0:T(4,128)S(1)}, u32[]{:S(2)}, u32[]{:S(2)}) collective-permute-start(f32[4,480]{1,0:T(4,128)S(1)} %bitcast.485), channel_id=1, source_target_pairs={{0,4},{4,0},{8,12},{12,8},{16,20},{20,16},{24,28},{28,24},{1,5},{5... | collective-permute-start | bytes 23048 | tf_op jit(solution)/shard_map/ppermute | solution.py:383
  383.5 3.2 collective-permute-start.13
  387.6 19.5 %all-to-all-start.7 = ((bf16[4,96,768]{2,1,0:T(8,128)(2,1)}), bf16[4,96,768]{2,1,0:T(8,128)(2,1)S(1)}, u32[]{:S(2)}, u32[]{:S(2)}) async-start(bf16[4,96,768]{2,1,0:T(8,128)(2,1)} %bitcast.104), calls=%async_computation.7 | async-start | bytes 1179648 | tf_op jit(solution)/shard_map/all_to_all | solution.py:642
  407.2 96.1 %all-to-all-start.6 = ((bf16[8,192,768]{2,1,0:T(8,128)(2,1)}), bf16[8,192,768]{2,1,0:T(8,128)(2,1)}, u32[]{:S(2)}, u32[]{:S(2)}) async-start(bf16[8,192,768]{2,1,0:T(8,128)(2,1)} %maximum_bitcast_fusion), calls=%async_computation.6 | async-start | bytes 4718592 | tf_op jit(solution)/shard_map/all_to_all | solution.py:548
  413.3 45.3 %collective-permute-start.31 = (bf16[768,384]{1,0:T(8,128)(2,1)S(1)}, bf16[768,384]{1,0:T(8,128)(2,1)S(1)}, u32[]{:S(2)}, u32[]{:S(2)}) collective-permute-start(bf16[768,384]{1,0:T(8,128)(2,1)S(1)} %get-tuple-element.120), channel_id=1, source_target_pairs={{0,24},{4,28},{8,16},{12,20},{16,8},{20,12},{24,0},{28,4},{1,25},{... | collective-permute-start | bytes 1769480 | tf_op jit(solution)/shard_map/ppermute | solution.py:383
  416.3 37.6 %collective-permute-start.35 = (bf16[480]{0:T(512)(128)(2,1)S(1)}, bf16[480]{0:T(512)(128)(2,1)S(1)}, u32[]{:S(2)}, u32[]{:S(2)}) collective-permute-start(bf16[480]{0:T(512)(128)(2,1)S(1)} %get-tuple-element.91), channel_id=1, source_target_pairs={{0,24},{4,28},{8,16},{12,20},{16,8},{20,12},{24,0},{28,4},{1,25},{... | collective-permute-start | bytes 2888 | tf_op jit(solution)/shard_map/ppermute | solution.py:383
  416.4 39.3 %collective-permute-start.34 = (bf16[480]{0:T(512)(128)(2,1)S(1)}, bf16[480]{0:T(512)(128)(2,1)S(1)}, u32[]{:S(2)}, u32[]{:S(2)}) collective-permute-start(bf16[480]{0:T(512)(128)(2,1)S(1)} %get-tuple-element.92), channel_id=1, source_target_pairs={{0,16},{4,20},{8,24},{12,28},{16,0},{20,4},{24,8},{28,12},{1,17},{... | collective-permute-start | bytes 2888 | tf_op jit(solution)/shard_map/ppermute | solution.py:383
  418.4 38.7 %collective-permute-start.33 = (bf16[480]{0:T(512)(128)(2,1)S(1)}, bf16[480]{0:T(512)(128)(2,1)S(1)}, u32[]{:S(2)}, u32[]{:S(2)}) collective-permute-start(bf16[480]{0:T(512)(128)(2,1)S(1)} %get-tuple-element.90), channel_id=1, source_target_pairs={{0,8},{4,12},{8,0},{12,4},{16,24},{20,28},{24,16},{28,20},{1,9},{5... | collective-permute-start | bytes 2888 | tf_op jit(solution)/shard_map/ppermute | solution.py:383
  419.9 46.1 %collective-permute-start.30 = (bf16[768,384]{1,0:T(8,128)(2,1)S(1)}, bf16[768,384]{1,0:T(8,128)(2,1)S(1)}, u32[]{:S(2)}, u32[]{:S(2)}) collective-permute-start(bf16[768,384]{1,0:T(8,128)(2,1)S(1)} %get-tuple-element.121), channel_id=1, source_target_pairs={{0,16},{4,20},{8,24},{12,28},{16,0},{20,4},{24,8},{28,12},{1,17},{... | collective-permute-start | bytes 1769480 | tf_op jit(solution)/shard_map/ppermute | solution.py:383
  453.9 16.3 %collective-permute-start.29 = (bf16[768,384]{1,0:T(8,128)(2,1)S(1)}, bf16[768,384]{1,0:T(8,128)(2,1)S(1)}, u32[]{:S(2)}, u32[]{:S(2)}) collective-permute-start(bf16[768,384]{1,0:T(8,128)(2,1)S(1)} %get-tuple-element.119), channel_id=1, source_target_pairs={{0,8},{4,12},{8,0},{12,4},{16,24},{20,28},{24,16},{28,20},{1,9},{5... | collective-permute-start | bytes 1769480 | tf_op jit(solution)/shard_map/ppermute | solution.py:383
  455.7 27.2 %collective-permute-start.39 = (bf16[384,768]{1,0:T(8,128)(2,1)}, bf16[384,768]{1,0:T(8,128)(2,1)}, u32[]{:S(2)}, u32[]{:S(2)}) collective-permute-start(bf16[384,768]{1,0:T(8,128)(2,1)} %get-tuple-element.117), channel_id=1, source_target_pairs={{0,24},{4,28},{8,16},{12,20},{16,8},{20,12},{24,0},{28,4},{1,25},{... | collective-permute-start | bytes 1769480 | tf_op jit(solution)/shard_map/ppermute | solution.py:383
  457.1 33.7 %collective-permute-start.38 = (bf16[384,768]{1,0:T(8,128)(2,1)}, bf16[384,768]{1,0:T(8,128)(2,1)}, u32[]{:S(2)}, u32[]{:S(2)}) collective-permute-start(bf16[384,768]{1,0:T(8,128)(2,1)} %get-tuple-element.118), channel_id=1, source_target_pairs={{0,16},{4,20},{8,24},{12,28},{16,0},{20,4},{24,8},{28,12},{1,17},{... | collective-permute-start | bytes 1769480 | tf_op jit(solution)/shard_map/ppermute | solution.py:383
  458.6 35.5 %collective-permute-start.37 = (bf16[384,768]{1,0:T(8,128)(2,1)}, bf16[384,768]{1,0:T(8,128)(2,1)}, u32[]{:S(2)}, u32[]{:S(2)}) collective-permute-start(bf16[384,768]{1,0:T(8,128)(2,1)} %get-tuple-element.116), channel_id=1, source_target_pairs={{0,8},{4,12},{8,0},{12,4},{16,24},{20,28},{24,16},{28,20},{1,9},{5... | collective-permute-start | bytes 1769480 | tf_op jit(solution)/shard_map/ppermute | solution.py:383
  472.6 24.4 %collective-permute-start.20 = (bf16[96,768]{1,0:T(8,128)(2,1)S(1)}, bf16[96,768]{1,0:T(8,128)(2,1)S(1)}, u32[]{:S(2)}, u32[]{:S(2)}) collective-permute-start(bf16[96,768]{1,0:T(8,128)(2,1)S(1)} %reduce_sum.242), channel_id=1, source_target_pairs={{0,3},{1,2},{2,1},{3,0},{4,7},{5,6},{6,5},{7,4},{8,11},{9,10},{10,... | collective-permute-start | bytes 442376 | tf_op jit(solution)/shard_map/ppermute | solution.py:383
  474.1 22.9 %collective-permute-start.19 = (bf16[96,768]{1,0:T(8,128)(2,1)S(1)}, bf16[96,768]{1,0:T(8,128)(2,1)S(1)}, u32[]{:S(2)}, u32[]{:S(2)}) collective-permute-start(bf16[96,768]{1,0:T(8,128)(2,1)S(1)} %reduce_sum.242), channel_id=1, source_target_pairs={{0,2},{1,3},{2,0},{3,1},{4,6},{5,7},{6,4},{7,5},{8,10},{9,11},{10,... | collective-permute-start | bytes 442376 | tf_op jit(solution)/shard_map/ppermute | solution.py:383
  482.9 14.1 %collective-permute-start.18 = (bf16[96,768]{1,0:T(8,128)(2,1)S(1)}, bf16[96,768]{1,0:T(8,128)(2,1)S(1)}, u32[]{:S(2)}, u32[]{:S(2)}) collective-permute-start(bf16[96,768]{1,0:T(8,128)(2,1)S(1)} %reduce_sum.242), channel_id=1, source_target_pairs={{0,1},{1,0},{2,3},{3,2},{4,5},{5,4},{6,7},{7,6},{8,9},{9,8},{10,11... | collective-permute-start | bytes 442376 | tf_op jit(solution)/shard_map/ppermute | solution.py:383
  499.8 17.6 %collective-permute-start.21 = (bf16[384,768]{1,0:T(8,128)(2,1)}, bf16[384,768]{1,0:T(8,128)(2,1)}, u32[]{:S(2)}, u32[]{:S(2)}) collective-permute-start(bf16[384,768]{1,0:T(8,128)(2,1)} %bitcast_select_fusion.2), channel_id=1, source_target_pairs={{0,4},{4,0},{8,12},{12,8},{16,20},{20,16},{24,28},{28,24},{1,5},{5... | collective-permute-start | bytes 1769480 | tf_op jit(solution)/shard_map/ppermute | solution.py:383
  499.8 16.4 %collective-permute-start.22 = (bf16[384,768]{1,0:T(8,128)(2,1)}, bf16[384,768]{1,0:T(8,128)(2,1)}, u32[]{:S(2)}, u32[]{:S(2)}) collective-permute-start(bf16[384,768]{1,0:T(8,128)(2,1)} %bitcast_select_fusion.2), channel_id=1, source_target_pairs={{0,8},{4,12},{8,0},{12,4},{16,24},{20,28},{24,16},{28,20},{1,9},{5... | collective-permute-start | bytes 1769480 | tf_op jit(solution)/shard_map/ppermute | solution.py:383
  500.4 28.4 %collective-permute-start.24 = (bf16[384,768]{1,0:T(8,128)(2,1)}, bf16[384,768]{1,0:T(8,128)(2,1)}, u32[]{:S(2)}, u32[]{:S(2)}) collective-permute-start(bf16[384,768]{1,0:T(8,128)(2,1)} %bitcast_select_fusion.2), channel_id=1, source_target_pairs={{0,16},{4,20},{8,24},{12,28},{16,0},{20,4},{24,8},{28,12},{1,17},{... | collective-permute-start | bytes 1769480 | tf_op jit(solution)/shard_map/ppermute | solution.py:383
  500.9 27.9 %collective-permute-start.26 = (bf16[384,768]{1,0:T(8,128)(2,1)}, bf16[384,768]{1,0:T(8,128)(2,1)}, u32[]{:S(2)}, u32[]{:S(2)}) collective-permute-start(bf16[384,768]{1,0:T(8,128)(2,1)} %bitcast_select_fusion.2), channel_id=1, source_target_pairs={{0,24},{4,28},{8,16},{12,20},{16,8},{20,12},{24,0},{28,4},{1,25},{... | collective-permute-start | bytes 1769480 | tf_op jit(solution)/shard_map/ppermute | solution.py:383
  513.1 3.9 collective-permute-start.8
  516.2 21.5 %collective-permute-start.23 = (bf16[384,768]{1,0:T(8,128)(2,1)}, bf16[384,768]{1,0:T(8,128)(2,1)S(1)}, u32[]{:S(2)}, u32[]{:S(2)}) collective-permute-start(bf16[384,768]{1,0:T(8,128)(2,1)} %collective-permute-done.22), channel_id=1, source_target_pairs={{0,4},{4,0},{8,12},{12,8},{16,20},{20,16},{24,28},{28,24},{1,5},{5... | collective-permute-start | bytes 1769480 | tf_op jit(solution)/shard_map/ppermute | solution.py:383
  517.0 4.8 collective-permute-start.9
  521.8 7.5 %collective-permute-start.10 = (f32[7,768]{1,0:T(8,128)S(1)}, f32[7,768]{1,0:T(8,128)S(1)}, u32[]{:S(2)}, u32[]{:S(2)}) collective-permute-start(f32[7,768]{1,0:T(8,128)S(1)} %add.485), channel_id=1, source_target_pairs={{0,4},{4,0},{8,12},{12,8},{16,20},{20,16},{24,28},{28,24},{1,5},{5... | collective-permute-start | bytes 64520 | tf_op jit(solution)/shard_map/ppermute | solution.py:383
  528.8 11.7 %collective-permute-start.25 = (bf16[384,768]{1,0:T(8,128)(2,1)}, bf16[384,768]{1,0:T(8,128)(2,1)S(1)}, u32[]{:S(2)}, u32[]{:S(2)}) collective-permute-start(bf16[384,768]{1,0:T(8,128)(2,1)} %collective-permute-done.24), channel_id=1, source_target_pairs={{0,4},{4,0},{8,12},{12,8},{16,20},{20,16},{24,28},{28,24},{1,5},{5... | collective-permute-start | bytes 1769480 | tf_op jit(solution)/shard_map/ppermute | solution.py:383
  528.8 14.5 %collective-permute-start.27 = (bf16[384,768]{1,0:T(8,128)(2,1)}, bf16[384,768]{1,0:T(8,128)(2,1)S(1)}, u32[]{:S(2)}, u32[]{:S(2)}) collective-permute-start(bf16[384,768]{1,0:T(8,128)(2,1)} %collective-permute-done.26), channel_id=1, source_target_pairs={{0,4},{4,0},{8,12},{12,8},{16,20},{20,16},{24,28},{28,24},{1,5},{5... | collective-permute-start | bytes 1769480 | tf_op jit(solution)/shard_map/ppermute | solution.py:383
  529.3 3.9 collective-permute-start.11
  533.2 3.8 collective-permute-start.12
  (68 other events, 715.1 us)
